TPU v7x, 512 devices: a whole 4x4x16 slice. The times are simulated.
512 devices in a mesh: row: 32 (over y, z_lo), width: 16 (over x, z_hi, core).
Axes of the slice: x: 4, y: 4, z: 16 (z_hi: 2, z_lo: 8; z = z_hi * 8 + z_lo), core: 2. Of those that a mesh axis runs over, the one named last changes fastest.
Arguments:
- store: bfloat16 [16384, 65536], P('row', 'width')
- queries: bfloat16 [32, 96, 65536], P('row', None, 'width')
- owner: int32 [4], replicated, may hold values from 0 to 31
Outputs:
- scores: float32 [4, 96, 16384], P(None, 'width', 'row')
Inputs may be any that keep to these rules, and one draw needn't show every extreme that they name: `owner`: index of a block of queries.
All inputs are finite; a program needn't handle non-finite values.
Results may differ from a plain program's by a relative error of at most 0.0003.
Values may be sent and summed in bfloat16 or wider, within the bound.
No kernel may reach another device: no remote copies, remote signals or barrier semaphores. Data moves between devices by JAX's collectives and lax.ppermute only.
A program may use at most 64 MiB of HBM per device.

v0:
```python
import math

import jax
import jax.numpy as jnp
from jax import lax
from jax.sharding import PartitionSpec as P

WIDTH = 65536


def broadcast(value, axis, source):
    kept = jnp.where(lax.axis_index(axis) == source, value, 0).astype(value.dtype)
    return lax.psum(kept, axis)


def square_sums(block):
    return jnp.sum(jnp.square(block.astype(jnp.float32)), axis=1)


def per_device(store, queries, owner):
    blocks = owner.shape[0]
    block_rows = queries.shape[1]
    share = block_rows // lax.axis_size("width")
    store_sq = square_sums(store)
    score_list = []
    square_list = []
    for index in range(blocks):
        chosen = broadcast(queries[0], "row", owner[index])
        inner = jnp.dot(chosen, store.T, preferred_element_type=jnp.float32)
        query_sq = square_sums(chosen)
        score_list.append(inner)
        square_list.append(query_sq)
    inners = jnp.stack(score_list)
    query_all = jnp.stack(square_list)
    inners = lax.psum_scatter(inners, "width", scatter_dimension=1, tiled=True)
    store_sq, query_all = lax.psum((store_sq, query_all), "width")
    query_all = lax.dynamic_slice_in_dim(query_all, lax.axis_index("width") * share, share, 1)
    query_scale = lax.rsqrt(query_all + 1e-06)[:, :, None]
    store_scale = lax.rsqrt(store_sq + 1e-06)[None, None, :]
    return inners * query_scale * store_scale * math.sqrt(WIDTH)


def solution(mesh):
    in_specs = (P("row", "width"), P("row", None, "width"), P())
    out_specs = P(None, "width", "row")
    return jax.shard_map(
        per_device, mesh=mesh, in_specs=in_specs, out_specs=out_specs, check_vma=False
    )
```

profile of v0, /device:TPU:1, one launch (start us, length us, event | category | flops | bytes accessed | tf_op | source)
XLA Modules:
  0.0 770.5 jit_solution(8435778704927737465)
XLA Ops:
  6.5 0.0 all-reduce.8.cloned.1.call-start
  6.5 1.5 fusion.2
  10.5 2.9 select_bitcast_fusion.3
  13.4 0.0 all-reduce.8.cloned.1.call-update
  13.5 0.0 all-reduce.6.cloned.1.call-start
  13.5 1.3 dynamic-slice
  15.4 3.1 multiply_reduce_fusion
  18.5 454.8 %all-reduce.8.cloned.1.call-done = (bf16[96,4096]{1,0:T(8,128)(2,1)}, bf16[96,4096]{1,0:T(8,128)(2,1)}, bf16[96,4096]{1,0:T(8,128)(2,1)}, bf16[96,4096]{1,0:T(8,128)(2,1)}) async-done(((bf16[96,4096]{1,0:T(8,128)(2,1)}, bf16[96,4096]{1,0:T(8,128)(2,1)}, bf16[96,4096]{1,0:T(8,128)(2,1)}, bf16[96,4096]{1,0:T(8,128)(2,1)}), (bf16[96,4096]{1,0:T(8,128)(2,1)}, bf16[96,4096]{1,0:T(8,128)(2,1)}, ...) | async-done | bytes 3145744 | tf_op jit(solution)/shard_map/psum | solution.py:13
  473.3 0.0 copy-start
  473.3 0.0 copy-start.2
  473.3 0.0 copy-start.3
  473.3 4.0 convolution_bitcast_fusion
  477.3 0.0 copy-done
  477.3 0.0 copy-done.2
  477.3 0.0 copy-start.4
  477.3 1.4 convolution_bitcast_fusion.1
  478.8 0.0 copy-done.3
  478.8 1.4 convolution_bitcast_fusion.2
  480.2 0.0 copy-done.4
  480.2 0.0 copy-start.1
  480.2 1.4 convolution_bitcast_fusion.3
  481.7 0.1 pad_maximum_fusion
  481.7 1.4 copy.5
  483.1 0.0 all-reduce.6.cloned.1.call-update
  483.1 0.4 multiply_reduce_fusion.3
  483.5 0.0 copy-done.1
  483.5 0.4 multiply_reduce_fusion.1
  484.0 82.6 %all-reduce.1 = (f32[512]{0:T(512)S(1)}, f32[4,96]{1,0:T(4,128)S(1)}) all-reduce(f32[512]{0:T(512)S(1)} %multiply_reduce_fusion, f32[4,96]{1,0:T(4,128)S(1)} %pad_maximum_fusion.1), channel_id=1, replica_groups=mesh['row'=32,'width'=16] {'width'}, use_global_device_ids=true, to_apply=%region_11.12 | all-reduce | flops 896 | bytes 7168 | tf_op jit(solution)/shard_map/psum | solution.py:36
  566.6 0.1 add_rsqrt_fusion.1
  566.7 0.1 copy.6
  566.8 195.4 %all-reduce.6.cloned.1.call-done = f32[4,96,512]{2,0,1:T(4,128)} async-done(((f32[4,96,512]{2,0,1:T(4,128)}), f32[4,96,512]{2,0,1:T(4,128)}) %all-reduce.6.cloned.1.call-update) | async-done | bytes 786448
  762.2 1.5 fusion.1
  (2 shorter events, 0.0 us)
Async XLA Ops:
  6.5 466.8 %all-reduce.8.cloned.1.call-start = ((), (), s32[]{:S(2)}) async-start(), calls=%async_computation.1 | async-start | bytes 6291456 | tf_op jit(solution)/shard_map/psum | solution.py:13
  13.5 748.7 %all-reduce.6.cloned.1.call-start = ((), (), s32[]{:S(2)}) async-start(), calls=%async_computation | async-start | bytes 1572864
  473.3 4.0 copy-start
  473.3 4.0 copy-start.2
  473.3 5.5 copy-start.3
  477.3 2.9 copy-start.4
  480.2 3.3 copy-start.1
Sparse Core Ops, SparseCore 0:
  13.6 459.6 all-reduce.7
  483.3 278.8 all-reduce.5
where the time goes:
time: 771 us
  waiting for transfers between devices  650 us (84%)
  blocking collectives  82.6 us (11%)
  between operations  16.7 us (2%)
  other arithmetic  8.43 us (1%)
  matrix products  8.26 us (1%)
    psum x1, waiting for transfers between devices, broadcast(): return lax.psum(kept, axis)  455 us
    unnamed x3, waiting for transfers between devices  195 us
    psum x1, blocking collectives, per_device(): store_sq, query_all = lax.psum((store_sq, query_all), 'width')  82.6 us
  transfers between devices with their start and end apart: 2, of which 2 were waited for; matrix products, arithmetic and copies ran while one was open for 1% of the time, Pallas kernels for 0%

commit v1 on v0

v1 whole, which is shorter than its diff:
```python
import math

import jax
import jax.numpy as jnp
from jax import lax
from jax.sharding import PartitionSpec as P

WIDTH = 65536
NY, NZ, NQ = 4, 8, 4
NX, NH, NC = 4, 2, 2
GROUPS_Y = [[y * NZ + z for y in range(NY)] for z in range(NZ)]
GROUPS_Q = [[y * NZ + h * NQ + k for k in range(NQ)] for y in range(NY) for h in range(2)]
GROUPS_XC = [[(x * NH + h) * NC + c for x in range(NX) for c in range(NC)] for h in range(NH)]
UP = [(y * NZ + z, (y + 1) % NY * NZ + z) for y in range(NY) for z in range(NZ)]
DOWN = [(b, a) for a, b in UP]
CROSS = [(r, r ^ NQ) for r in range(NY * NZ)]
SWAP_H = [(w, w ^ NC) for w in range(NX * NH * NC)]


def exchange(value, axis, groups):
    return lax.all_to_all(value, axis, 0, 0, axis_index_groups=groups)


def pick(parts, index):
    index = index.reshape((-1,) + (1,) * (parts.ndim - 2))
    out = parts[0]
    for k in range(1, parts.shape[0]):
        out = jnp.where(index == k, parts[k], out)
    return out


def spread(parts, owner, z):
    slots = owner.shape[0]
    _, rows, cols = parts.shape
    mine = pick(parts[:, None], owner // NZ)
    mine = mine.reshape(slots, NQ, rows // NQ, cols).transpose(1, 0, 2, 3)
    piece = pick(exchange(mine, "row", GROUPS_Q), owner % NQ)
    other = lax.ppermute(piece, "row", CROSS)
    here = (owner // NQ % 2 == z // NQ)[:, None, None]
    piece = jnp.where(here, piece, other)
    return exchange(jnp.broadcast_to(piece[None], (NQ,) + piece.shape), "row", GROUPS_Q)


def gather_y(mine):
    below = lax.ppermute(mine, "row", UP)
    above = lax.ppermute(mine, "row", DOWN)
    half = mine.shape[0] // 2
    far = jnp.concatenate(
        [lax.ppermute(below[:half], "row", UP), lax.ppermute(above[half:], "row", DOWN)]
    )
    return mine, below, above, far


def squares(block):
    return jnp.sum(jnp.square(block.astype(jnp.float32)), axis=-1)


def per_device(store, queries, owner):
    slots = owner.shape[0]
    rows, cols = queries.shape[1:]
    share = rows // (NX * NH * NC)
    y = lax.axis_index("row") // NZ
    z = lax.axis_index("row") % NZ
    quarter = cols // NY
    parts = queries[0].reshape(rows, NY, quarter).transpose(1, 0, 2)
    parts = exchange(parts, "row", GROUPS_Y)
    store_sq = squares(store)
    quarters = gather_y(spread(parts, owner, z))
    inner, query_sq = 0.0, 0.0
    for step, chosen in zip((0, -1, 1, 2), quarters):
        chosen = chosen.reshape(slots * rows, quarter)
        start = (y + step) % NY * quarter
        columns = lax.dynamic_slice_in_dim(store, start, quarter, 1)
        inner += lax.dot_general(
            chosen, columns, (((1,), (1,)), ((), ())), preferred_element_type=jnp.float32
        )
        query_sq += squares(chosen)
    def by_target(value):
        value = value.reshape(NX, slots, NH, NC, share, -1).transpose(0, 3, 2, 1, 4, 5)
        return value.reshape(NX * NC, NH, slots * share, -1)

    lanes = 128
    extra = jnp.zeros((slots * share, lanes), jnp.float32)
    extra = extra.at[:8, :64].set(store_sq.reshape(8, 64))
    extra = jnp.broadcast_to(extra, (NX * NC, NH, slots * share, lanes))
    extra = jnp.where(jnp.arange(lanes) == 64, by_target(query_sq), extra)
    total = jnp.concatenate([by_target(inner), extra], axis=3)
    total = jnp.sum(exchange(total, "width", GROUPS_XC), axis=0)
    h = lax.axis_index("width") // NC % NH
    keep = jnp.where(h == 0, total[0], total[1])
    give = jnp.where(h == 0, total[1], total[0])
    total = keep + lax.ppermute(give, "width", SWAP_H)
    depth = store.shape[0]
    store_sq = total[:8, depth : depth + 64].reshape(1, depth)
    query_sq = total[:, depth + 64 : depth + 65]
    scores = total[:, :depth] * lax.rsqrt(query_sq + 1e-06) * lax.rsqrt(store_sq + 1e-06)
    return (scores * math.sqrt(WIDTH)).reshape(slots, share, depth)


def solution(mesh):
    in_specs = (P("row", "width"), P("row", None, "width"), P())
    out_specs = P(None, "width", "row")
    return jax.shard_map(
        per_device, mesh=mesh, in_specs=in_specs, out_specs=out_specs, check_vma=False
    )
```

time: 771 us -> 172 us (0.22)
  waiting for transfers between devices: 650 us -> 72.7 us
  blocking collectives: 82.6 us -> 22.1 us
  starting transfers between devices: 0.04 us -> 54.5 us
  between operations: 16.7 us -> 0.34 us
    psum x1 -> x0, waiting for transfers between devices: 455 us -> none  [broadcast(): return lax.psum(kept, axis)]
    unnamed x3 -> x0, waiting for transfers between devices: 195 us -> none
    psum x1 -> x0, blocking collectives: 82.6 us -> none  [per_device(): store_sq, query_all = lax.psum((store_sq, query_all), 'width')]
    all_to_all x0 -> x3, waiting for transfers between devices: none -> 42.3 us  [exchange(): return lax.all_to_all(value, axis, 0, 0, axis_index_groups=groups)]
    ppermute x0 -> x6, starting transfers between devices: none -> 33.1 us  [the longest x1 11.3 us: per_device(): total = keep + lax.ppermute(give, 'width', SWAP_H)]
    ppermute x0 -> x6, waiting for transfers between devices: none -> 30.4 us  [the longest x1 15.5 us: spread(): other = lax.ppermute(piece, 'row', CROSS)]
    all_to_all x0 -> x1, blocking collectives: none -> 22.1 us  [exchange(): return lax.all_to_all(value, axis, 0, 0, axis_index_groups=groups)]
    all_to_all x0 -> x3, starting transfers between devices: none -> 21.4 us  [exchange(): return lax.all_to_all(value, axis, 0, 0, axis_index_groups=groups)]
  transfers between devices with their start and end apart: 2 -> 9, of which waited for: 2 -> 8; matrix products, arithmetic and copies ran while one was open for 1% -> 4% of each run, Pallas kernels for 0% -> 0%
where the time goes in v1:
time: 172 us; the launch traced here: 170 us
  waiting for transfers between devices  72.7 us (42%)
  starting transfers between devices  54.5 us (32%)
  blocking collectives  22.1 us (13%)
  other arithmetic  7.76 us (5%)
  matrix products  7.36 us (4%)
  local copies, waits for them, and re-layouts  5.54 us (3%)
    all_to_all x3, waiting for transfers between devices, exchange(): return lax.all_to_all(value, axis, 0, 0, axis_index_groups=groups)  42.3 us
    all_to_all x1, blocking collectives, exchange(): return lax.all_to_all(value, axis, 0, 0, axis_index_groups=groups)  22.1 us
    all_to_all x3, starting transfers between devices, exchange(): return lax.all_to_all(value, axis, 0, 0, axis_index_groups=groups)  21.4 us
    ppermute x1, waiting for transfers between devices, spread(): other = lax.ppermute(piece, 'row', CROSS)  15.5 us
    ppermute x1, starting transfers between devices, per_device(): total = keep + lax.ppermute(give, 'width', SWAP_H)  11.3 us
    ppermute x1, waiting for transfers between devices, gather_y(): below = lax.ppermute(mine, 'row', UP)  10.8 us
    ppermute x1, starting transfers between devices, spread(): other = lax.ppermute(piece, 'row', CROSS)  8.82 us
    dot_general x4, matrix products, per_device(): lax.dot_general(chosen, columns, (((1,), (1,)), ((), ())), preferred_elem...  7.36 us
  transfers between devices with their start and end apart: 9, of which 8 were waited for; matrix products, arithmetic and copies ran while one was open for 4% of the time, Pallas kernels for 0%

profile of v1, /device:TPU:1, one launch (start us, length us, event | category | flops | bytes accessed | tf_op | source)
XLA Modules:
  0.0 170.3 jit_solution(4704922347041148952)
XLA Ops:
  0.0 2.3 %reshape_squeeze.3 = bf16[96,4,1024]{2,1,0:T(4,128)(2,1)S(1)} reshape(bf16[1,96,4096]{2,1,0:T(8,128)(2,1)} %param.6) | data formatting | bytes 1572864 | tf_op jit(solution)/shard_map/reshape;squeeze | solution.py:65
  2.3 1.1 copy.19
  3.4 5.0 %all-to-all-start = ((bf16[4,96,1024]{2,1,0:T(8,128)(2,1)}), bf16[4,96,1024]{2,1,0:T(8,128)(2,1)S(1)}, u32[]{:S(2)}, u32[]{:S(2)}) async-start(bf16[4,96,1024]{2,1,0:T(8,128)(2,1)} %copy.19), calls=%async_computation | async-start | bytes 1572864 | tf_op jit(solution)/shard_map/all_to_all | solution.py:21
  8.5 8.3 %all-to-all-done = bf16[4,96,1024]{2,1,0:T(8,128)(2,1)S(1)} async-done(((bf16[4,96,1024]{2,1,0:T(8,128)(2,1)}), bf16[4,96,1024]{2,1,0:T(8,128)(2,1)S(1)}, u32[]{:S(2)}, u32[]{:S(2)}) %all-to-all-start) | async-done | bytes 786464 | tf_op jit(solution)/shard_map/all_to_all | solution.py:21
  16.8 1.0 select_select_fusion
  17.9 8.7 %all-to-all-start.1 = ((bf16[4,4,24,1024]{3,2,1,0:T(8,128)(2,1)}), bf16[4,4,24,1024]{3,2,1,0:T(8,128)(2,1)S(1)}, u32[]{:S(2)}, u32[]{:S(2)}) async-start(bf16[4,4,24,1024]{3,2,1,0:T(8,128)(2,1)} %select_select_fusion), calls=%async_computation.1 | async-start | bytes 1572864 | tf_op jit(solution)/shard_map/all_to_all | solution.py:21
  26.5 19.6 %all-to-all-done.1 = bf16[4,4,24,1024]{3,2,1,0:T(8,128)(2,1)S(1)} async-done(((bf16[4,4,24,1024]{3,2,1,0:T(8,128)(2,1)}), bf16[4,4,24,1024]{3,2,1,0:T(8,128)(2,1)S(1)}, u32[]{:S(2)}, u32[]{:S(2)}) %all-to-all-start.1) | async-done | bytes 786464 | tf_op jit(solution)/shard_map/all_to_all | solution.py:21
  46.2 8.8 %collective-permute-start = (bf16[4,24,1024]{2,1,0:T(8,128)(2,1)S(1)}, bf16[4,24,1024]{2,1,0:T(8,128)(2,1)S(1)}, u32[]{:S(2)}, u32[]{:S(2)}) collective-permute-start(bf16[4,24,1024]{2,1,0:T(8,128)(2,1)S(1)} %fusion.9), channel_id=1, source_target_pairs={{0,64},{16,80},{32,96},{48,112},{64,0},{80,16},{96,32},{112,48},{1... | collective-permute-start | bytes 589832 | tf_op jit(solution)/shard_map/ppermute | solution.py:38
  55.1 15.5 %collective-permute-done = bf16[4,24,1024]{2,1,0:T(8,128)(2,1)S(1)} collective-permute-done((bf16[4,24,1024]{2,1,0:T(8,128)(2,1)S(1)}, bf16[4,24,1024]{2,1,0:T(8,128)(2,1)S(1)}, u32[]{:S(2)}, u32[]{:S(2)}) %collective-permute-start) | collective-permute-done | bytes 196640 | tf_op jit(solution)/shard_map/ppermute | solution.py:38
  70.8 22.1 %all_to_all.20 = bf16[4,4,24,1024]{3,2,1,0:T(8,128)(2,1)S(1)} all-to-all(bf16[4,4,24,1024]{3,2,1,0:T(8,128)(2,1)S(1)} %broadcast_in_dim.122), channel_id=1, replica_groups={{0,16,32,48},{64,80,96,112},{128,144,160,176},{192,208,224,240},{256,27..., dimensions={0} | all-to-all | bytes 1572864 | tf_op jit(solution)/shard_map/all_to_all | solution.py:21
  92.9 2.2 %collective-permute-start.1 = (bf16[4,4,24,1024]{3,2,1,0:T(8,128)(2,1)S(1)}, bf16[4,4,24,1024]{3,2,1,0:T(8,128)(2,1)S(1)}, u32[]{:S(2)}, u32[]{:S(2)}) collective-permute-start(bf16[4,4,24,1024]{3,2,1,0:T(8,128)(2,1)S(1)} %all_to_all.20), channel_id=1, source_target_pairs={{0,128},{16,144},{32,160},{48,176},{64,192},{80,208},{96,224},{112... | collective-permute-start | bytes 2359304 | tf_op jit(solution)/shard_map/ppermute | solution.py:45
  95.1 4.3 %collective-permute-start.2 = (bf16[4,4,24,1024]{3,2,1,0:T(8,128)(2,1)S(1)}, bf16[4,4,24,1024]{3,2,1,0:T(8,128)(2,1)S(1)}, u32[]{:S(2)}, u32[]{:S(2)}) collective-permute-start(bf16[4,4,24,1024]{3,2,1,0:T(8,128)(2,1)S(1)} %all_to_all.20), channel_id=1, source_target_pairs={{128,0},{144,16},{160,32},{176,48},{192,64},{208,80},{224,96},{240... | collective-permute-start | bytes 2359304 | tf_op jit(solution)/shard_map/ppermute | solution.py:46
  99.5 3.1 %multiply_reduce_fusion = f32[512]{0:T(512)S(1)} fusion(bf16[512,4096]{1,0:T(8,128)(2,1)} %param.5), kind=kLoop, calls=%fused_computation | loop fusion | flops 6290944 | bytes 4196352 | tf_op jit(solution)/shard_map/reduce_sum | solution.py:55
  102.9 10.8 %collective-permute-done.1 = bf16[4,4,24,1024]{3,2,1,0:T(8,128)(2,1)S(1)} collective-permute-done((bf16[4,4,24,1024]{3,2,1,0:T(8,128)(2,1)S(1)}, bf16[4,4,24,1024]{3,2,1,0:T(8,128)(2,1)S(1)}, u32[]{:S(2)}, u32[]{:S(2)}) %collective-permute-start.1) | collective-permute-done | bytes 786464 | tf_op jit(solution)/shard_map/ppermute | solution.py:45
  113.8 1.9 %collective-permute-start.3 = (bf16[2,4,24,1024]{3,2,1,0:T(8,128)(2,1)S(1)}, bf16[2,4,24,1024]{3,2,1,0:T(8,128)(2,1)S(1)}, u32[]{:S(2)}, u32[]{:S(2)}) collective-permute-start(bf16[2,4,24,1024]{3,2,1,0:T(8,128)(2,1)S(1)} %slice.94), channel_id=1, source_target_pairs={{0,128},{16,144},{32,160},{48,176},{64,192},{80,208},{96,224},{112... | collective-permute-start | bytes 1179656 | tf_op jit(solution)/shard_map/ppermute | solution.py:49
  115.7 4.6 %collective-permute-start.4 = (bf16[2,4,24,1024]{3,2,1,0:T(8,128)(2,1)S(1)}, bf16[2,4,24,1024]{3,2,1,0:T(8,128)(2,1)S(1)}, u32[]{:S(2)}, u32[]{:S(2)}) collective-permute-start(bf16[2,4,24,1024]{3,2,1,0:T(8,128)(2,1)S(1)} %slice.95), channel_id=1, source_target_pairs={{128,0},{144,16},{160,32},{176,48},{192,64},{208,80},{224,96},{240... | collective-permute-start | bytes 1179656 | tf_op jit(solution)/shard_map/ppermute | solution.py:49
  120.3 1.8 %fusion.4 = f32[384,512]{1,0:T(8,128)S(1)} fusion(bf16[384,1024]{1,0:T(8,128)(2,1)S(1)} %bitcast.60, bf16[512,4096]{1,0:T(8,128)(2,1)} %param.5, s32[]{:T(128)S(6)} %select_n.139), kind=kOutput, calls=%fused_computation.11 | convolution fusion | flops 402653184 | bytes 2621444 | tf_op jit(solution)/shard_map/dot_general | solution.py:74
  122.4 0.2 multiply_reduce_fusion.3
  122.6 1.8 %convolution_add_fusion.1 = f32[384,512]{1,0:T(8,128)S(1)} fusion(f32[384,512]{1,0:T(8,128)S(1)} %fusion.4, bf16[384,1024]{1,0:T(8,128)(2,1)S(1)} %bitcast.58, bf16[512,4096]{1,0:T(8,128)(2,1)} %param.5, s32[]{:T(128)S(6)} %select_n.137), kind=kOutput, calls=%fused_computation.6 | convolution fusion | flops 402849792 | bytes 3407876 | tf_op jit(solution)/shard_map/dot_general | solution.py:74
  124.5 0.8 collective-permute-done.3
  125.3 0.9 collective-permute-done.4
  126.8 1.8 %fusion.1 = f32[384,512]{1,0:T(8,128)S(1)} fusion(bf16[384,1024]{1,0:T(8,128)(2,1)S(1)} %bitcast.61, bf16[512,4096]{1,0:T(8,128)(2,1)} %param.5, s32[]{:T(128)S(6)} %select_n.143), kind=kOutput, calls=%fused_computation.8 | convolution fusion | flops 402653184 | bytes 2621444 | tf_op jit(solution)/shard_map/dot_general | solution.py:74
  128.6 1.9 %fusion = f32[384,512]{1,0:T(8,128)S(1)} fusion(f32[384,512]{1,0:T(8,128)S(1)} %fusion.1, f32[384,512]{1,0:T(8,128)S(1)} %convolution_add_fusion.1, bf16[384,1024]{1,0:T(8,128)(2,1)S(1)} %bitcast.59, bf16[512,4096]{1,0:T(8,128)(2,1)} %param.5, s32[]{:T(128)S(6)} %select_n.141), kind=kOutput, calls=%fused_computation.7 | convolution fusion | flops 403046400 | bytes 4194308 | tf_op jit(solution)/shard_map/dot_general | solution.py:74
  130.6 0.6 copy.20
  131.2 0.3 broadcast_select_fusion.1
  131.5 1.4 pad_maximum_fusion
  132.9 7.7 %all-to-all-start.3 = ((f32[8,2,24,640]{3,1,2,0:T(2,128)}), f32[8,2,24,640]{3,1,2,0:T(2,128)S(1)}, u32[]{:S(2)}, u32[]{:S(2)}) async-start(f32[8,2,24,640]{3,1,2,0:T(2,128)} %pad_maximum_fusion), calls=%async_computation.3 | async-start | bytes 1966080 | tf_op jit(solution)/shard_map/all_to_all | solution.py:21
  140.7 14.4 %all-to-all-done.3 = f32[8,2,24,640]{3,1,2,0:T(2,128)S(1)} async-done(((f32[8,2,24,640]{3,1,2,0:T(2,128)}), f32[8,2,24,640]{3,1,2,0:T(2,128)S(1)}, u32[]{:S(2)}, u32[]{:S(2)}) %all-to-all-start.3) | async-done | bytes 983072 | tf_op jit(solution)/shard_map/all_to_all | solution.py:21
  155.1 0.4 reduce_sum.59
  155.6 11.3 %collective-permute-start.5 = (f32[24,640]{1,0:T(8,128)S(1)}, f32[24,640]{1,0:T(8,128)S(1)}, u32[]{:S(2)}, u32[]{:S(2)}) collective-permute-start(f32[24,640]{1,0:T(8,128)S(1)} %bitcast.70), channel_id=1, source_target_pairs={{0,2},{1,3},{2,0},{3,1},{4,6},{5,7},{6,4},{7,5},{8,10},{9,11},{10,... | collective-permute-start | bytes 184328 | tf_op jit(solution)/shard_map/ppermute | solution.py:92
  166.9 2.4 %collective-permute-done.5 = f32[24,640]{1,0:T(8,128)S(1)} collective-permute-done((f32[24,640]{1,0:T(8,128)S(1)}, f32[24,640]{1,0:T(8,128)S(1)}, u32[]{:S(2)}, u32[]{:S(2)}) %collective-permute-start.5) | collective-permute-done | bytes 61472 | tf_op jit(solution)/shard_map/ppermute | solution.py:92
  169.7 0.7 copy.27
  (34 shorter events, 2.2 us)
Async XLA Ops:
  0.0 8.4 %copy-start = (s32[4]{0:T(128)S(1)}, s32[4]{0:T(128)}, u32[]{:S(2)}) copy-start(s32[4]{0:T(128)} %param.7) | copy-start | bytes 52
  3.4 13.4 %all-to-all-start = ((bf16[4,96,1024]{2,1,0:T(8,128)(2,1)}), bf16[4,96,1024]{2,1,0:T(8,128)(2,1)S(1)}, u32[]{:S(2)}, u32[]{:S(2)}) async-start(bf16[4,96,1024]{2,1,0:T(8,128)(2,1)} %copy.19), calls=%async_computation | async-start | bytes 1572864 | tf_op jit(solution)/shard_map/all_to_all | solution.py:21
  17.9 28.3 %all-to-all-start.1 = ((bf16[4,4,24,1024]{3,2,1,0:T(8,128)(2,1)}), bf16[4,4,24,1024]{3,2,1,0:T(8,128)(2,1)S(1)}, u32[]{:S(2)}, u32[]{:S(2)}) async-start(bf16[4,4,24,1024]{3,2,1,0:T(8,128)(2,1)} %select_select_fusion), calls=%async_computation.1 | async-start | bytes 1572864 | tf_op jit(solution)/shard_map/all_to_all | solution.py:21
  46.2 24.3 %collective-permute-start = (bf16[4,24,1024]{2,1,0:T(8,128)(2,1)S(1)}, bf16[4,24,1024]{2,1,0:T(8,128)(2,1)S(1)}, u32[]{:S(2)}, u32[]{:S(2)}) collective-permute-start(bf16[4,24,1024]{2,1,0:T(8,128)(2,1)S(1)} %fusion.9), channel_id=1, source_target_pairs={{0,64},{16,80},{32,96},{48,112},{64,0},{80,16},{96,32},{112,48},{1... | collective-permute-start | bytes 589832 | tf_op jit(solution)/shard_map/ppermute | solution.py:38
  92.9 20.8 %collective-permute-start.1 = (bf16[4,4,24,1024]{3,2,1,0:T(8,128)(2,1)S(1)}, bf16[4,4,24,1024]{3,2,1,0:T(8,128)(2,1)S(1)}, u32[]{:S(2)}, u32[]{:S(2)}) collective-permute-start(bf16[4,4,24,1024]{3,2,1,0:T(8,128)(2,1)S(1)} %all_to_all.20), channel_id=1, source_target_pairs={{0,128},{16,144},{32,160},{48,176},{64,192},{80,208},{96,224},{112... | collective-permute-start | bytes 2359304 | tf_op jit(solution)/shard_map/ppermute | solution.py:45
  95.1 20.6 %collective-permute-start.2 = (bf16[4,4,24,1024]{3,2,1,0:T(8,128)(2,1)S(1)}, bf16[4,4,24,1024]{3,2,1,0:T(8,128)(2,1)S(1)}, u32[]{:S(2)}, u32[]{:S(2)}) collective-permute-start(bf16[4,4,24,1024]{3,2,1,0:T(8,128)(2,1)S(1)} %all_to_all.20), channel_id=1, source_target_pairs={{128,0},{144,16},{160,32},{176,48},{192,64},{208,80},{224,96},{240... | collective-permute-start | bytes 2359304 | tf_op jit(solution)/shard_map/ppermute | solution.py:46
  113.8 11.5 %collective-permute-start.3 = (bf16[2,4,24,1024]{3,2,1,0:T(8,128)(2,1)S(1)}, bf16[2,4,24,1024]{3,2,1,0:T(8,128)(2,1)S(1)}, u32[]{:S(2)}, u32[]{:S(2)}) collective-permute-start(bf16[2,4,24,1024]{3,2,1,0:T(8,128)(2,1)S(1)} %slice.94), channel_id=1, source_target_pairs={{0,128},{16,144},{32,160},{48,176},{64,192},{80,208},{96,224},{112... | collective-permute-start | bytes 1179656 | tf_op jit(solution)/shard_map/ppermute | solution.py:49
  115.7 10.4 %collective-permute-start.4 = (bf16[2,4,24,1024]{3,2,1,0:T(8,128)(2,1)S(1)}, bf16[2,4,24,1024]{3,2,1,0:T(8,128)(2,1)S(1)}, u32[]{:S(2)}, u32[]{:S(2)}) collective-permute-start(bf16[2,4,24,1024]{3,2,1,0:T(8,128)(2,1)S(1)} %slice.95), channel_id=1, source_target_pairs={{128,0},{144,16},{160,32},{176,48},{192,64},{208,80},{224,96},{240... | collective-permute-start | bytes 1179656 | tf_op jit(solution)/shard_map/ppermute | solution.py:49
  132.9 22.1 %all-to-all-start.3 = ((f32[8,2,24,640]{3,1,2,0:T(2,128)}), f32[8,2,24,640]{3,1,2,0:T(2,128)S(1)}, u32[]{:S(2)}, u32[]{:S(2)}) async-start(f32[8,2,24,640]{3,1,2,0:T(2,128)} %pad_maximum_fusion), calls=%async_computation.3 | async-start | bytes 1966080 | tf_op jit(solution)/shard_map/all_to_all | solution.py:21
  155.6 13.7 %collective-permute-start.5 = (f32[24,640]{1,0:T(8,128)S(1)}, f32[24,640]{1,0:T(8,128)S(1)}, u32[]{:S(2)}, u32[]{:S(2)}) collective-permute-start(f32[24,640]{1,0:T(8,128)S(1)} %bitcast.70), channel_id=1, source_target_pairs={{0,2},{1,3},{2,0},{3,1},{4,6},{5,7},{6,4},{7,5},{8,10},{9,11},{10,... | collective-permute-start | bytes 184328 | tf_op jit(solution)/shard_map/ppermute | solution.py:92

commit v2 on v0

v2 whole, which is shorter than its diff:
```python
import math

import jax
import jax.numpy as jnp
from jax import lax
from jax.experimental import pallas as pl
from jax.experimental.pallas import tpu as pltpu
from jax.sharding import PartitionSpec as P

WIDTH = 65536
NY, NZ, NQ = 4, 8, 4
NX, NH, NC = 4, 2, 2
NW = NX * NH * NC
EXTRA = 8
QUADS = [[y * NZ + h * NQ + k for k in range(NQ)] for y in range(NY) for h in range(2)]
SQUARES = [[y * NZ + h * NQ + k for y in range(NY) for k in range(NQ)] for h in range(2)]
PLANES = [
    [(y * NZ + z) * NW + (x * NH + h) * NC + c for y in range(NY) for x in range(NX)]
    for z in range(NZ) for h in range(NH) for c in range(NC)
]
CROSS = [(r, r ^ NQ) for r in range(NY * NZ)]
SWAP_C = [(w, w ^ 1) for w in range(NW)]
SWAP_H = [(w, w ^ NC) for w in range(NW)]


def turn(step):
    return [(y * NZ + z, (y + step) % NY * NZ + z) for y in range(NY) for z in range(NZ)]


def cut_kernel(block, out):
    width = out.shape[2]
    for part in range(out.shape[0]):
        out[part] = block[:, part * width : (part + 1) * width]


def cut_columns(block, parts):
    rows, cols = block.shape
    vmem = pl.BlockSpec(memory_space=pltpu.VMEM)
    return pl.pallas_call(
        cut_kernel,
        in_specs=[vmem],
        out_specs=vmem,
        out_shape=jax.ShapeDtypeStruct((parts, rows, cols // parts), block.dtype),
    )(block)


def products_kernel(y, chosen, store_sq, *refs):
    stores, (first, second), (blocks, done) = refs[:NY], refs[NY : NY + 2], refs[NY + 2 :]
    copies = [
        pltpu.make_async_copy(stores[step], blocks.at[step], done.at[step]) for step in range(NY)
    ]
    for copy in copies:
        copy.start()
    parts, rows, width = chosen.shape
    depth = store_sq.shape[1]
    few = second.shape[3]
    query_sq = jnp.zeros((EXTRA, rows), jnp.float32)
    ones = jnp.ones((EXTRA, width), jnp.bfloat16)
    for k in range(parts):
        square = jnp.square(chosen[k].astype(jnp.float32))
        high = square.astype(jnp.bfloat16)
        low = (square - high.astype(jnp.float32)).astype(jnp.bfloat16)
        for part in (high, low):
            query_sq += lax.dot_general(
                ones, part, (((1,), (1,)), ((), ())), preferred_element_type=jnp.float32
            )
    place = lax.broadcasted_iota(jnp.int32, (EXTRA, depth), 0)
    for step in range(NY):
        copies[step].wait()
        inner = 0.0
        for k in range(parts):
            inner += lax.dot_general(
                chosen[k], blocks[step, :, k * width : (k + 1) * width],
                (((1,), (1,)), ((), ())), preferred_element_type=jnp.float32,
            )
        target = lax.rem(y[0] + (NY - step), NY)
        for group, out in ((0, first), (1, second)):
            for side in range(NC):
                for x in range(NX):
                    at = ((group * NC + side) * NX + x) * few
                    out[side, pl.ds(target, 1), x, :few] = inner[None, at : at + few]
        for side in range(NC):
            for x in range(NX):
                extra = jnp.zeros((EXTRA, depth), jnp.float32)
                if step == 0:
                    extra = jnp.where(place == 0, store_sq[...], extra)
                for group in range(NH):
                    at = ((group * NC + side) * NX + x) * few
                    line = jnp.concatenate(
                        [query_sq[:, at : at + few], jnp.zeros((EXTRA, depth - few), jnp.float32)], axis=1
                    )
                    extra = jnp.where(place == group + 1, line, extra)
                first[side, pl.ds(target, 1), x, few:] = extra[None]


def products(y, chosen, store_sq, stores):
    parts, m, k = chosen.shape
    n = stores[0].shape[0]
    few = m // (NH * NC * NX)
    vmem = pl.BlockSpec(memory_space=pltpu.VMEM)
    return pl.pallas_call(
        products_kernel,
        in_specs=[pl.BlockSpec(memory_space=pltpu.SMEM), vmem, vmem]
        + [pl.BlockSpec(memory_space=pl.ANY)] * NY,
        out_specs=[vmem, vmem],
        out_shape=[
            jax.ShapeDtypeStruct((NC, NY, NX, few + EXTRA, n), jnp.float32),
            jax.ShapeDtypeStruct((NC, NY, NX, few, n), jnp.float32),
        ],
        scratch_shapes=[
            pltpu.VMEM((NY, n, parts * k), stores[0].dtype),
            pltpu.SemaphoreType.DMA((NY,)),
        ],
        compiler_params=pltpu.CompilerParams(vmem_limit_bytes=28 << 20),
        cost_estimate=pl.CostEstimate(
            flops=2 * NY * m * n * parts * k, bytes_accessed=NY * n * (parts * k * 2 + m * 4), transcendentals=0
        ),
    )(y.reshape(1), chosen, store_sq.reshape(1, n), *stores)


def squares(block):
    return jnp.sum(jnp.square(block.astype(jnp.float32)), axis=-1)


def per_device(store, queries, owner):
    slots = owner.shape[0]
    rows, cols = queries.shape[1:]
    depth = store.shape[0]
    share = rows // NW
    y = lax.axis_index("row") // NZ
    half = lax.axis_index("row") % NZ // NQ
    w = lax.axis_index("width")
    h, c = w // NC % NH, w % NC
    quarter = cols // NY
    parts = cut_columns(queries[0], NY * NQ)
    parts = lax.all_to_all(parts, "row", 0, 0, axis_index_groups=SQUARES)

    stores = []
    for step in range(NY):
        part = lax.dynamic_slice_in_dim(store, (y + step) % NY * quarter, quarter, 1)
        stores.append(lax.ppermute(part, "row", turn(step)) if step else part)

    row = jnp.arange(slots * rows)
    slot = row // share % slots
    x = row // (share * slots) % NX
    to_c = c ^ 1 ^ row // (share * slots * NX) % NC
    to_h = h ^ 1 ^ row // (share * slots * NX * NC)
    inside = ((x * NH + to_h) * NC + to_c) * share + row % share
    of_row = jnp.sum(jnp.where(slot[:, None] == jnp.arange(slots), owner, 0), axis=1)
    source = (of_row // NZ * NQ + of_row % NQ) * rows + inside
    one_hot = (source[:, None] == jnp.arange(NY * NQ * rows)).astype(parts.dtype)
    piece = jnp.dot(
        one_hot, parts.reshape(NY * NQ * rows, -1), preferred_element_type=jnp.float32
    ).astype(parts.dtype)
    other = lax.ppermute(piece, "row", CROSS)
    piece = jnp.where((of_row // NQ % 2 == half)[:, None], piece, other)
    chosen = lax.all_gather(piece, "row", axis_index_groups=QUADS)

    def summed(parts):
        give, keep = parts
        total = keep + lax.ppermute(give, "width", SWAP_C)
        total = total.reshape((NY * NX,) + total.shape[2:])
        total = lax.all_to_all(total, ("row", "width"), 0, 0, axis_index_groups=PLANES)
        return jnp.sum(total, axis=0)

    first, second = products(y, chosen, squares(store), stores)
    give, keep = summed(first), summed(second)
    few = slots * share
    got = lax.ppermute(give, "width", SWAP_H)
    total = keep + got[:few]
    store_sq = give[few] + got[few]
    query_sq = give[few + 2, :few] + got[few + 1, :few]
    scores = total * lax.rsqrt(query_sq + 1e-06)[:, None] * lax.rsqrt(store_sq + 1e-06)
    return (scores * math.sqrt(WIDTH)).reshape(slots, share, depth)


def solution(mesh):
    in_specs = (P("row", "width"), P("row", None, "width"), P())
    out_specs = P(None, "width", "row")
    return jax.shard_map(
        per_device, mesh=mesh, in_specs=in_specs, out_specs=out_specs, check_vma=False
    )
```

time: 771 us -> 132 us (0.17)
  waiting for transfers between devices: 650 us -> 36.6 us
  blocking collectives: 82.6 us -> 16.1 us
  starting transfers between devices: 0.04 us -> 56.2 us
  between operations: 16.7 us -> 0.35 us
    psum x1 -> x0, waiting for transfers between devices: 455 us -> none  [broadcast(): return lax.psum(kept, axis)]
    unnamed x3 -> x0, waiting for transfers between devices: 195 us -> none
    psum x1 -> x0, blocking collectives: 82.6 us -> none  [per_device(): store_sq, query_all = lax.psum((store_sq, query_all), 'width')]
    ppermute x0 -> x7, starting transfers between devices: none -> 36 us  [the longest x1 11 us: per_device(): got = lax.ppermute(give, 'width', SWAP_H)]
    all_to_all x0 -> x3, starting transfers between devices: none -> 20.3 us  [the longest x2 11.1 us: summed(): lax.all_to_all(total, ('row', 'width'), 0, 0, axis_index_groups=PLANES)]
    all_to_all x0 -> x3, waiting for transfers between devices: none -> 20 us  [the longest x2 16.1 us: summed(): lax.all_to_all(total, ('row', 'width'), 0, 0, axis_index_groups=PLANES)]
    ppermute x0 -> x7, waiting for transfers between devices: none -> 16.6 us  [the longest x1 15.3 us: per_device(): other = lax.ppermute(piece, 'row', CROSS)]
    all_gather x0 -> x1, blocking collectives: none -> 16.1 us  [per_device(): chosen = lax.all_gather(piece, 'row', axis_index_groups=QUADS)]
  transfers between devices with their start and end apart: 2 -> 10, of which waited for: 2 -> 6; matrix products, arithmetic and copies ran while one was open for 1% -> 9% of each run, Pallas kernels for 0% -> 0%
where the time goes in v2:
time: 132 us; the launch traced here: 131 us
  starting transfers between devices  56.2 us (43%)
  waiting for transfers between devices  36.6 us (28%)
  blocking collectives  16.1 us (12%)
  local copies, waits for them, and re-layouts  6.98 us (5%)
  other arithmetic  6.91 us (5%)
  Pallas kernels  6.79 us (5%)
    all_gather x1, blocking collectives, per_device(): chosen = lax.all_gather(piece, 'row', axis_index_groups=QUADS)  16.1 us
    all_to_all x2, waiting for transfers between devices, summed(): lax.all_to_all(total, ('row', 'width'), 0, 0, axis_index_groups=PLANES)  16.1 us
    ppermute x1, waiting for transfers between devices, per_device(): other = lax.ppermute(piece, 'row', CROSS)  15.3 us
    all_to_all x2, starting transfers between devices, summed(): lax.all_to_all(total, ('row', 'width'), 0, 0, axis_index_groups=PLANES)  11.1 us
    ppermute x1, starting transfers between devices, per_device(): got = lax.ppermute(give, 'width', SWAP_H)  11 us
    ppermute x3, starting transfers between devices, per_device(): stores.append(lax.ppermute(part, 'row', turn(step)) if step else part)  9.95 us
    all_to_all x1, starting transfers between devices, per_device(): parts = lax.all_to_all(parts, 'row', 0, 0, axis_index_groups=SQUARES)  9.19 us
    ppermute x1, starting transfers between devices, per_device(): other = lax.ppermute(piece, 'row', CROSS)  8.87 us
  transfers between devices with their start and end apart: 10, of which 6 were waited for; matrix products, arithmetic and copies ran while one was open for 9% of the time, Pallas kernels for 0%

profile of v2, /device:TPU:1, one launch (start us, length us, event | category | flops | bytes accessed | tf_op | source)
XLA Modules:
  0.0 130.5 jit_solution(7288935523104274860)
XLA Ops:
  0.0 2.1 %shard_map.37 = bf16[16,96,256]{2,1,0:T(8,128)(2,1)} custom-call(bf16[96,4096]{1,0:T(8,128)(2,1)} %bitcast.21), custom_call_target="tpu_custom_call" | custom-call | tf_op jit(solution)/shard_map/pallas_call | solution.py:39
  2.1 9.2 %all-to-all-start = ((bf16[16,96,256]{2,1,0:T(8,128)(2,1)}), bf16[16,96,256]{2,1,0:T(8,128)(2,1)S(1)}, u32[]{:S(2)}, u32[]{:S(2)}) async-start(bf16[16,96,256]{2,1,0:T(8,128)(2,1)} %shard_map.37), calls=%async_computation | async-start | bytes 1572864 | tf_op jit(solution)/shard_map/all_to_all | solution.py:136
  11.4 4.0 %constant_dynamic-slice_fusion.3 = (bf16[512,1024]{1,0:T(8,128)(2,1)}, bf16[512,1024]{1,0:T(8,128)(2,1)}, bf16[512,1024]{1,0:T(8,128)(2,1)S(1)}, bf16[512,1024]{1,0:T(8,128)(2,1)}) fusion(bf16[512,4096]{1,0:T(8,128)(2,1)} %param.3, s32[]{:T(128)S(6)} %select_n.182, s32[]{:T(128)S(6)} %select_n.178, s32[]{:T(128)S(6)} %select_n.176, s32[]{:T(128)S(6)} %select_n.180), kind=kLoop, calls=%fused_computation.86 | loop fusion | bytes 8388624 | tf_op jit(solution)/shard_map/dynamic_slice | solution.py:140
  15.4 4.4 %collective-permute-start.3 = (bf16[512,1024]{1,0:T(8,128)(2,1)}, bf16[512,1024]{1,0:T(8,128)(2,1)S(1)}, u32[]{:S(2)}, u32[]{:S(2)}) collective-permute-start(bf16[512,1024]{1,0:T(8,128)(2,1)} %get-tuple-element.9), channel_id=1, source_target_pairs={{0,384},{16,400},{32,416},{48,432},{64,448},{80,464},{96,480},{112... | collective-permute-start | bytes 3145736 | tf_op jit(solution)/shard_map/ppermute | solution.py:141
  19.8 1.9 %collective-permute-start.1 = (bf16[512,1024]{1,0:T(8,128)(2,1)}, bf16[512,1024]{1,0:T(8,128)(2,1)}, u32[]{:S(2)}, u32[]{:S(2)}) collective-permute-start(bf16[512,1024]{1,0:T(8,128)(2,1)} %get-tuple-element.10), channel_id=1, source_target_pairs={{0,128},{16,144},{32,160},{48,176},{64,192},{80,208},{96,224},{112... | collective-permute-start | bytes 3145736 | tf_op jit(solution)/shard_map/ppermute | solution.py:141
  21.7 3.7 %collective-permute-start.2 = (bf16[512,1024]{1,0:T(8,128)(2,1)}, bf16[512,1024]{1,0:T(8,128)(2,1)}, u32[]{:S(2)}, u32[]{:S(2)}) collective-permute-start(bf16[512,1024]{1,0:T(8,128)(2,1)} %get-tuple-element.12), channel_id=1, source_target_pairs={{0,256},{16,272},{32,288},{48,304},{64,320},{80,336},{96,352},{112... | collective-permute-start | bytes 3145736 | tf_op jit(solution)/shard_map/ppermute | solution.py:141
  25.4 0.1 select_reduce_fusion
  25.5 3.1 %multiply_reduce_fusion = f32[512]{0:T(512)S(1)} fusion(bf16[512,4096]{1,0:T(8,128)(2,1)} %param.3), kind=kLoop, calls=%fused_computation | loop fusion | flops 6290944 | bytes 4196352 | tf_op jit(solution)/shard_map/reduce_sum | solution.py:122
  28.6 4.0 %all-to-all-done = bf16[16,96,256]{2,1,0:T(8,128)(2,1)S(1)} async-done(((bf16[16,96,256]{2,1,0:T(8,128)(2,1)}), bf16[16,96,256]{2,1,0:T(8,128)(2,1)S(1)}, u32[]{:S(2)}, u32[]{:S(2)}) %all-to-all-start) | async-done | bytes 786464 | tf_op jit(solution)/shard_map/all_to_all | solution.py:136
  32.6 0.6 fusion.2
  33.2 8.9 %collective-permute-start = (bf16[384,256]{1,0:T(8,128)(2,1)S(1)}, bf16[384,256]{1,0:T(8,128)(2,1)S(1)}, u32[]{:S(2)}, u32[]{:S(2)}) collective-permute-start(bf16[384,256]{1,0:T(8,128)(2,1)S(1)} %fusion.2), channel_id=1, source_target_pairs={{0,64},{16,80},{32,96},{48,112},{64,0},{80,16},{96,32},{112,48},{1... | collective-permute-start | bytes 589832 | tf_op jit(solution)/shard_map/ppermute | solution.py:155
  42.1 15.3 %collective-permute-done = bf16[384,256]{1,0:T(8,128)(2,1)S(1)} collective-permute-done((bf16[384,256]{1,0:T(8,128)(2,1)S(1)}, bf16[384,256]{1,0:T(8,128)(2,1)S(1)}, u32[]{:S(2)}, u32[]{:S(2)}) %collective-permute-start) | collective-permute-done | bytes 196640 | tf_op jit(solution)/shard_map/ppermute | solution.py:155
  57.4 0.1 broadcast_select_fusion
  57.5 16.1 %all-gather = bf16[1536,256]{1,0:T(8,128)(2,1)S(1)} all-gather(bf16[384,256]{1,0:T(8,128)(2,1)S(1)} %broadcast_select_fusion), channel_id=2, replica_groups={{0,16,32,48},{64,80,96,112},{128,144,160,176},{192,208,224,240},{256,27..., dimensions={0}, use_global_device_ids=true | all-gather | bytes 983040 | tf_op jit(solution)/shard_map/all_gather | solution.py:157
  73.7 1.0 copy-done
  74.6 1.2 copy-done.1
  75.9 4.7 %shard_map.38 = (f32[2,4,4,32,512]{4,3,2,1,0:T(8,128)S(1)}, f32[2,4,4,24,512]{4,3,2,1,0:T(8,128)S(1)}) custom-call(s32[1]{0:T(128)} %bitcast.y, bf16[4,384,256]{2,1,0:T(8,128)(2,1)S(1)} %bitcast.19, f32[1,512]{1,0:T(1,128)S(1)} %bitcast.20, bf16[512,1024]{1,0:T(8,128)(2,1)S(1)} %get-tuple-element.11.refs_0_, ...), custom_call_target="tpu_custom_call" | custom-call | flops 1610612736 | bytes 7340032 | tf_op jit(solution)/shard_map/pallas_call | solution.py:101
  80.6 0.1 slice_bitcast_fusion
  80.6 4.3 %collective-permute-start.5 = (f32[4,4,32,512]{3,2,1,0:T(8,128)S(1)}, f32[4,4,32,512]{3,2,1,0:T(8,128)S(1)}, u32[]{:S(2)}, u32[]{:S(2)}) collective-permute-start(f32[4,4,32,512]{3,2,1,0:T(8,128)S(1)} %slice_bitcast_fusion), channel_id=1, source_target_pairs={{0,1},{1,0},{2,3},{3,2},{4,5},{5,4},{6,7},{7,6},{8,9},{9,8},{10,11... | collective-permute-start | bytes 3145736 | tf_op jit(solution)/shard_map/ppermute | solution.py:161
  85.0 1.9 %collective-permute-start.4 = (f32[4,4,24,512]{3,2,1,0:T(8,128)S(1)}, f32[4,4,24,512]{3,2,1,0:T(8,128)}, u32[]{:S(2)}, u32[]{:S(2)}) collective-permute-start(f32[4,4,24,512]{3,2,1,0:T(8,128)S(1)} %slice_bitcast_fusion.1), channel_id=1, source_target_pairs={{0,1},{1,0},{2,3},{3,2},{4,5},{5,4},{6,7},{7,6},{8,9},{9,8},{10,11... | collective-permute-start | bytes 2359304 | tf_op jit(solution)/shard_map/ppermute | solution.py:161
  86.9 0.3 collective-permute-done.5
  87.2 1.2 bitcast_add_fusion
  88.4 6.6 %all-to-all-start.2 = ((f32[16,32,512]{2,1,0:T(8,128)}), f32[16,32,512]{2,1,0:T(8,128)S(1)}, u32[]{:S(2)}, u32[]{:S(2)}) async-start(f32[16,32,512]{2,1,0:T(8,128)} %bitcast.10), calls=%async_computation.2 | async-start | bytes 2097152 | tf_op jit(solution)/shard_map/all_to_all | solution.py:163
  95.0 2.2 %bitcast_add_fusion.1 = f32[4,4,24,512]{3,2,1,0:T(8,128)} fusion(f32[4,4,24,512]{3,2,1,0:T(8,128)} %collective-permute-done.4, f32[2,4,4,24,512]{4,3,2,1,0:T(8,128)S(1)} %get-tuple-element.7), kind=kLoop, calls=%fused_computation.7 | loop fusion | flops 196608 | bytes 2359296 | tf_op jit(solution)/shard_map/add | solution.py:161
  97.1 14.2 %all-to-all-done.2 = f32[16,32,512]{2,1,0:T(8,128)S(1)} async-done(((f32[16,32,512]{2,1,0:T(8,128)}), f32[16,32,512]{2,1,0:T(8,128)S(1)}, u32[]{:S(2)}, u32[]{:S(2)}) %all-to-all-start.2) | async-done | bytes 1048608 | tf_op jit(solution)/shard_map/all_to_all | solution.py:163
  111.3 4.5 %all-to-all-start.1 = ((f32[16,24,512]{2,1,0:T(8,128)}), f32[16,24,512]{2,1,0:T(8,128)S(1)}, u32[]{:S(2)}, u32[]{:S(2)}) async-start(f32[16,24,512]{2,1,0:T(8,128)} %bitcast.7), calls=%async_computation.1 | async-start | bytes 1572864 | tf_op jit(solution)/shard_map/all_to_all | solution.py:163
  115.8 0.1 reduce_sum.39
  115.9 11.0 %collective-permute-start.6 = (f32[32,512]{1,0:T(8,128)S(1)}, f32[32,512]{1,0:T(8,128)S(1)}, u32[]{:S(2)}, u32[]{:S(2)}) collective-permute-start(f32[32,512]{1,0:T(8,128)S(1)} %reduce_sum.39), channel_id=1, source_target_pairs={{0,2},{1,3},{2,0},{3,1},{4,6},{5,7},{6,4},{7,5},{8,10},{9,11},{10,... | collective-permute-start | bytes 196616 | tf_op jit(solution)/shard_map/ppermute | solution.py:169
  126.8 1.9 %all-to-all-done.1 = f32[16,24,512]{2,1,0:T(8,128)S(1)} async-done(((f32[16,24,512]{2,1,0:T(8,128)}), f32[16,24,512]{2,1,0:T(8,128)S(1)}, u32[]{:S(2)}, u32[]{:S(2)}) %all-to-all-start.1) | async-done | bytes 786464 | tf_op jit(solution)/shard_map/all_to_all | solution.py:163
  128.8 1.0 collective-permute-done.6
  129.8 0.1 fusion.5
  129.9 0.7 copy.5
  (16 shorter events, 0.2 us)
Async XLA Ops:
  2.1 30.5 %all-to-all-start = ((bf16[16,96,256]{2,1,0:T(8,128)(2,1)}), bf16[16,96,256]{2,1,0:T(8,128)(2,1)S(1)}, u32[]{:S(2)}, u32[]{:S(2)}) async-start(bf16[16,96,256]{2,1,0:T(8,128)(2,1)} %shard_map.37), calls=%async_computation | async-start | bytes 1572864 | tf_op jit(solution)/shard_map/all_to_all | solution.py:136
  11.4 14.0 %copy-start.2 = (s32[4]{0:T(128)S(1)}, s32[4]{0:T(128)}, u32[]{:S(2)}) copy-start(s32[4]{0:T(128)} %param.5) | copy-start | bytes 52
  15.4 58.3 %collective-permute-start.3 = (bf16[512,1024]{1,0:T(8,128)(2,1)}, bf16[512,1024]{1,0:T(8,128)(2,1)S(1)}, u32[]{:S(2)}, u32[]{:S(2)}) collective-permute-start(bf16[512,1024]{1,0:T(8,128)(2,1)} %get-tuple-element.9), channel_id=1, source_target_pairs={{0,384},{16,400},{32,416},{48,432},{64,448},{80,464},{96,480},{112... | collective-permute-start | bytes 3145736 | tf_op jit(solution)/shard_map/ppermute | solution.py:141
  19.8 54.9 %collective-permute-start.1 = (bf16[512,1024]{1,0:T(8,128)(2,1)}, bf16[512,1024]{1,0:T(8,128)(2,1)}, u32[]{:S(2)}, u32[]{:S(2)}) collective-permute-start(bf16[512,1024]{1,0:T(8,128)(2,1)} %get-tuple-element.10), channel_id=1, source_target_pairs={{0,128},{16,144},{32,160},{48,176},{64,192},{80,208},{96,224},{112... | collective-permute-start | bytes 3145736 | tf_op jit(solution)/shard_map/ppermute | solution.py:141
  21.7 52.9 %collective-permute-start.2 = (bf16[512,1024]{1,0:T(8,128)(2,1)}, bf16[512,1024]{1,0:T(8,128)(2,1)}, u32[]{:S(2)}, u32[]{:S(2)}) collective-permute-start(bf16[512,1024]{1,0:T(8,128)(2,1)} %get-tuple-element.12), channel_id=1, source_target_pairs={{0,256},{16,272},{32,288},{48,304},{64,320},{80,336},{96,352},{112... | collective-permute-start | bytes 3145736 | tf_op jit(solution)/shard_map/ppermute | solution.py:141
  33.2 24.2 %collective-permute-start = (bf16[384,256]{1,0:T(8,128)(2,1)S(1)}, bf16[384,256]{1,0:T(8,128)(2,1)S(1)}, u32[]{:S(2)}, u32[]{:S(2)}) collective-permute-start(bf16[384,256]{1,0:T(8,128)(2,1)S(1)} %fusion.2), channel_id=1, source_target_pairs={{0,64},{16,80},{32,96},{48,112},{64,0},{80,16},{96,32},{112,48},{1... | collective-permute-start | bytes 589832 | tf_op jit(solution)/shard_map/ppermute | solution.py:155
  73.7 1.0 copy-start
  74.6 1.2 copy-start.1
  80.6 6.6 %collective-permute-start.5 = (f32[4,4,32,512]{3,2,1,0:T(8,128)S(1)}, f32[4,4,32,512]{3,2,1,0:T(8,128)S(1)}, u32[]{:S(2)}, u32[]{:S(2)}) collective-permute-start(f32[4,4,32,512]{3,2,1,0:T(8,128)S(1)} %slice_bitcast_fusion), channel_id=1, source_target_pairs={{0,1},{1,0},{2,3},{3,2},{4,5},{5,4},{6,7},{7,6},{8,9},{9,8},{10,11... | collective-permute-start | bytes 3145736 | tf_op jit(solution)/shard_map/ppermute | solution.py:161
  85.0 9.9 %collective-permute-start.4 = (f32[4,4,24,512]{3,2,1,0:T(8,128)S(1)}, f32[4,4,24,512]{3,2,1,0:T(8,128)}, u32[]{:S(2)}, u32[]{:S(2)}) collective-permute-start(f32[4,4,24,512]{3,2,1,0:T(8,128)S(1)} %slice_bitcast_fusion.1), channel_id=1, source_target_pairs={{0,1},{1,0},{2,3},{3,2},{4,5},{5,4},{6,7},{7,6},{8,9},{9,8},{10,11... | collective-permute-start | bytes 2359304 | tf_op jit(solution)/shard_map/ppermute | solution.py:161
  88.4 22.9 %all-to-all-start.2 = ((f32[16,32,512]{2,1,0:T(8,128)}), f32[16,32,512]{2,1,0:T(8,128)S(1)}, u32[]{:S(2)}, u32[]{:S(2)}) async-start(f32[16,32,512]{2,1,0:T(8,128)} %bitcast.10), calls=%async_computation.2 | async-start | bytes 2097152 | tf_op jit(solution)/shard_map/all_to_all | solution.py:163
  111.3 17.5 %all-to-all-start.1 = ((f32[16,24,512]{2,1,0:T(8,128)}), f32[16,24,512]{2,1,0:T(8,128)S(1)}, u32[]{:S(2)}, u32[]{:S(2)}) async-start(f32[16,24,512]{2,1,0:T(8,128)} %bitcast.7), calls=%async_computation.1 | async-start | bytes 1572864 | tf_op jit(solution)/shard_map/all_to_all | solution.py:163
  115.9 13.9 %collective-permute-start.6 = (f32[32,512]{1,0:T(8,128)S(1)}, f32[32,512]{1,0:T(8,128)S(1)}, u32[]{:S(2)}, u32[]{:S(2)}) collective-permute-start(f32[32,512]{1,0:T(8,128)S(1)} %reduce_sum.39), channel_id=1, source_target_pairs={{0,2},{1,3},{2,0},{3,1},{4,6},{5,7},{6,4},{7,5},{8,10},{9,11},{10,... | collective-permute-start | bytes 196616 | tf_op jit(solution)/shard_map/ppermute | solution.py:169

commit v3 on v2

v3 whole, which is shorter than its diff:
```python
import math

import jax
import jax.numpy as jnp
from jax import lax
from jax.experimental import pallas as pl
from jax.experimental.pallas import tpu as pltpu
from jax.sharding import PartitionSpec as P

WIDTH = 65536
NY, NZ, NQ = 4, 8, 4
NX, NH, NC = 4, 2, 2
NW = NX * NH * NC
LANES = 128
EXTRA = 8
QUADS = [[y * NZ + h * NQ + k for k in range(NQ)] for y in range(NY) for h in range(2)]
SQUARES = [[y * NZ + h * NQ + k for y in range(NY) for k in range(NQ)] for h in range(2)]
PLANES = [
    [(y * NZ + z) * NW + (x * NH + h) * NC + c for y in range(NY) for x in range(NX)]
    for z in range(NZ) for h in range(NH) for c in range(NC)
]
CROSS = [(r, r ^ NQ) for r in range(NY * NZ)]
SWAP_C = [(w, w ^ 1) for w in range(NW)]
SWAP_H = [(w, w ^ NC) for w in range(NW)]


def turn(step):
    return [(y * NZ + z, (y + step) % NY * NZ + z) for y in range(NY) for z in range(NZ)]


def cut_kernel(block, out):
    width = out.shape[2]
    for part in range(out.shape[0]):
        out[part] = block[:, part * width : (part + 1) * width]


def cut_columns(block, parts):
    rows, cols = block.shape
    vmem = pl.BlockSpec(memory_space=pltpu.VMEM)
    return pl.pallas_call(
        cut_kernel,
        in_specs=[vmem],
        out_specs=vmem,
        out_shape=jax.ShapeDtypeStruct((parts, rows, cols // parts), block.dtype),
    )(block)


def products_kernel(y, chosen, store_sq, *refs):
    stores, outs, (queries, blocks, done) = refs[:NY], refs[NY : NY + NH * NC], refs[NY + NH * NC :]
    copies = [pltpu.make_async_copy(chosen, queries, done.at[NY])] + [
        pltpu.make_async_copy(stores[step], blocks.at[step], done.at[step]) for step in range(NY)
    ]
    for copy in copies:
        copy.start()
    parts, rows, width = queries.shape
    few = rows // (NH * NC * NX)
    tiles = outs[-1].shape[2] // few
    copies[0].wait()
    query_sq = jnp.zeros((EXTRA, rows), jnp.float32)
    ones = jnp.ones((EXTRA, width), jnp.bfloat16)
    for k in range(parts):
        square = jnp.square(queries[k].astype(jnp.float32))
        high = square.astype(jnp.bfloat16)
        low = (square - high.astype(jnp.float32)).astype(jnp.bfloat16)
        for part in (high, low):
            query_sq += lax.dot_general(
                ones, part, (((1,), (1,)), ((), ())), preferred_element_type=jnp.float32
            )
    place = lax.broadcasted_iota(jnp.int32, (EXTRA, LANES), 0)
    for step in range(NY):
        copies[1 + step].wait()
        inner = 0.0
        for k in range(parts):
            inner += lax.dot_general(
                queries[k], blocks[step, :, k * width : (k + 1) * width],
                (((1,), (1,)), ((), ())), preferred_element_type=jnp.float32,
            )
        target = lax.rem(y[0] + (NY - step), NY)
        for side, out in enumerate(outs):
            for x in range(NX):
                at = (side * NX + x) * few
                for tile in range(tiles):
                    out[pl.ds(target, 1), x, tile * few : (tile + 1) * few] = inner[
                        None, at : at + few, tile * LANES : (tile + 1) * LANES
                    ]
        for side, out in enumerate(outs[:NC]):
            for x in range(NX):
                extra = store_sq[...] if step == 0 else jnp.zeros((EXTRA, LANES), jnp.float32)
                for group in range(NH):
                    at = ((group * NC + side) * NX + x) * few
                    line = jnp.concatenate(
                        [query_sq[:, at : at + few], jnp.zeros((EXTRA, LANES - few), jnp.float32)], axis=1
                    )
                    extra = jnp.where(place == tiles + group, line, extra)
                out[pl.ds(target, 1), x, tiles * few :] = extra[None]


def products(y, chosen, store_sq, stores):
    parts, m, k = chosen.shape
    n = stores[0].shape[0]
    few = m // (NH * NC * NX)
    height = n // LANES * few
    extra = jnp.pad(store_sq.reshape(n // LANES, LANES), ((0, EXTRA - n // LANES), (0, 0)))
    vmem, anywhere = pl.BlockSpec(memory_space=pltpu.VMEM), pl.BlockSpec(memory_space=pl.ANY)
    outs = pl.pallas_call(
        products_kernel,
        in_specs=[pl.BlockSpec(memory_space=pltpu.SMEM), anywhere, vmem] + [anywhere] * NY,
        out_specs=[vmem] * (NH * NC),
        out_shape=[
            jax.ShapeDtypeStruct((NY, NX, height + more, LANES), jnp.float32)
            for more in (EXTRA, 0) for _ in range(NC)
        ],
        scratch_shapes=[
            pltpu.VMEM((parts, m, k), chosen.dtype),
            pltpu.VMEM((NY, n, parts * k), stores[0].dtype),
            pltpu.SemaphoreType.DMA((NY + 1,)),
        ],
        compiler_params=pltpu.CompilerParams(vmem_limit_bytes=24 << 20),
        cost_estimate=pl.CostEstimate(
            flops=2 * NY * m * n * parts * k, bytes_accessed=NY * n * (parts * k * 2 + m * 4), transcendentals=0
        ),
    )(y.reshape(1), chosen, extra, *stores)
    return outs[:NC], outs[NC:]


def squares(block):
    return jnp.sum(jnp.square(block.astype(jnp.float32)), axis=-1)


def per_device(store, queries, owner):
    slots = owner.shape[0]
    rows, cols = queries.shape[1:]
    depth = store.shape[0]
    share = rows // NW
    y = lax.axis_index("row") // NZ
    half = lax.axis_index("row") % NZ // NQ
    w = lax.axis_index("width")
    h, c = w // NC % NH, w % NC
    quarter = cols // NY
    parts = cut_columns(queries[0], NY * NQ)
    parts = lax.all_to_all(parts, "row", 0, 0, axis_index_groups=SQUARES)

    stores = []
    for step in range(NY):
        part = lax.dynamic_slice_in_dim(store, (y + step) % NY * quarter, quarter, 1)
        stores.append(lax.ppermute(part, "row", turn(step)) if step else part)

    row = jnp.arange(slots * rows)
    slot = row % slots
    x = row // (share * slots) % NX
    to_c = c ^ 1 ^ row // (share * slots * NX) % NC
    to_h = h ^ 1 ^ row // (share * slots * NX * NC)
    inside = ((x * NH + to_h) * NC + to_c) * share + row // slots % share
    of_row = jnp.sum(jnp.where(slot[:, None] == jnp.arange(slots), owner, 0), axis=1)
    source = (of_row // NZ * NQ + of_row % NQ) * rows + inside
    one_hot = (source[:, None] == jnp.arange(NY * NQ * rows)).astype(parts.dtype)
    piece = jnp.dot(
        one_hot, parts.reshape(NY * NQ * rows, -1), preferred_element_type=jnp.float32
    ).astype(parts.dtype)
    other = lax.ppermute(piece, "row", CROSS)
    piece, store = lax.optimization_barrier((piece, store))
    store_sq = squares(store)
    piece = jnp.where((of_row // NQ % 2 == half)[:, None], piece, other)
    chosen = lax.all_gather(piece, "row", axis_index_groups=QUADS)

    def summed(parts):
        give, keep = parts
        total = keep + lax.ppermute(give, "width", SWAP_C)
        total = total.reshape((NY * NX,) + total.shape[2:])
        total = lax.all_to_all(total, ("row", "width"), 0, 0, axis_index_groups=PLANES)
        return jnp.sum(total, axis=0)

    first, second = products(y, chosen, store_sq, stores)
    give, keep = summed(first), summed(second)
    got = lax.ppermute(give, "width", SWAP_H)
    tiles, few = depth // LANES, slots * share
    height = tiles * few
    store_sq = (give + got)[height : height + tiles, None, None, :]
    query_sq = give[height + tiles + 1, :few] + got[height + tiles, :few]
    scores = (keep + got[:height]).reshape(tiles, share, slots, LANES)
    scores = scores * lax.rsqrt(query_sq + 1e-06).reshape(share, slots, 1)
    scores = scores * lax.rsqrt(store_sq + 1e-06) * math.sqrt(WIDTH)
    return scores.transpose(2, 1, 0, 3).reshape(slots, share, depth)


def solution(mesh):
    in_specs = (P("row", "width"), P("row", None, "width"), P())
    out_specs = P(None, "width", "row")
    return jax.shard_map(
        per_device, mesh=mesh, in_specs=in_specs, out_specs=out_specs, check_vma=False
    )
```

time: 132 us -> 128 us (0.970)
  waiting for transfers between devices: 36.6 us -> 34.5 us
  local copies, waits for them, and re-layouts: 6.98 us -> 4.93 us
  other arithmetic: 6.91 us -> 5.57 us
    all_to_all x2, waiting for transfers between devices: 16.1 us -> 10.2 us  [summed(): lax.all_to_all(total, ('row', 'width'), 0, 0, axis_index_groups=PLANES)]
    ppermute x2, waiting for transfers between devices: 0.27 us -> 4.08 us  [summed(): total = keep + lax.ppermute(give, 'width', SWAP_C)]
    ppermute x1, waiting for transfers between devices: 15.3 us -> 12.3 us  [per_device(): other = lax.ppermute(piece, 'row', CROSS)]
    all_to_all x1, waiting for transfers between devices: 3.97 us -> 6.94 us  [per_device(): parts = lax.all_to_all(parts, 'row', 0, 0, axis_index_groups=SQUARES)]
    unnamed x6 -> x4, local copies, waits for them, and re-layouts: 2.2 us -> 0.01 us
    add x2, other arithmetic: 3.34 us -> 2.01 us  [summed(): total = keep + lax.ppermute(give, 'width', SWAP_C)]
  transfers between devices with their start and end apart: 10 -> 10, of which waited for: 6 -> 7; matrix products, arithmetic and copies ran while one was open for 9% -> 8% of each run, Pallas kernels for 0% -> 0%
where the time goes in v3:
time: 128 us; the launch traced here: 126 us
  starting transfers between devices  56.1 us (44%)
  waiting for transfers between devices  34.5 us (27%)
  blocking collectives  16.1 us (13%)
  Pallas kernels  6.87 us (5%)
  other arithmetic  5.57 us (4%)
  local copies, waits for them, and re-layouts  4.93 us (4%)
  matrix products  1.7 us (1%)
    all_gather x1, blocking collectives, per_device(): chosen = lax.all_gather(piece, 'row', axis_index_groups=QUADS)  16.1 us
    ppermute x1, waiting for transfers between devices, per_device(): other = lax.ppermute(piece, 'row', CROSS)  12.3 us
    ppermute x1, starting transfers between devices, per_device(): got = lax.ppermute(give, 'width', SWAP_H)  11 us
    all_to_all x2, starting transfers between devices, summed(): lax.all_to_all(total, ('row', 'width'), 0, 0, axis_index_groups=PLANES)  10.4 us
    all_to_all x2, waiting for transfers between devices, summed(): lax.all_to_all(total, ('row', 'width'), 0, 0, axis_index_groups=PLANES)  10.2 us
    ppermute x3, starting transfers between devices, per_device(): stores.append(lax.ppermute(part, 'row', turn(step)) if step else part)  9.9 us
    all_to_all x1, starting transfers between devices, per_device(): parts = lax.all_to_all(parts, 'row', 0, 0, axis_index_groups=SQUARES)  9.23 us
    ppermute x1, starting transfers between devices, per_device(): other = lax.ppermute(piece, 'row', CROSS)  8.87 us
  transfers between devices with their start and end apart: 10, of which 7 were waited for; matrix products, arithmetic and copies ran while one was open for 8% of the time, Pallas kernels for 0%

profile of v3, /device:TPU:1, one launch (start us, length us, event | category | flops | bytes accessed | tf_op | source)
XLA Modules:
  0.0 126.0 jit_solution(12918270259221991923)
XLA Ops:
  0.0 2.1 %shard_map.37 = bf16[16,96,256]{2,1,0:T(8,128)(2,1)} custom-call(bf16[96,4096]{1,0:T(8,128)(2,1)} %bitcast.15), custom_call_target="tpu_custom_call" | custom-call | tf_op jit(solution)/shard_map/pallas_call | solution.py:40
  2.1 9.2 %all-to-all-start = ((bf16[16,96,256]{2,1,0:T(8,128)(2,1)}), bf16[16,96,256]{2,1,0:T(8,128)(2,1)}, u32[]{:S(2)}, u32[]{:S(2)}) async-start(bf16[16,96,256]{2,1,0:T(8,128)(2,1)} %shard_map.37), calls=%async_computation | async-start | bytes 1572864 | tf_op jit(solution)/shard_map/all_to_all | solution.py:141
  11.4 0.0 copy-start.1
  11.5 4.2 %constant_dynamic-slice_fusion.3 = (bf16[512,1024]{1,0:T(8,128)(2,1)}, bf16[512,1024]{1,0:T(8,128)(2,1)}, bf16[512,1024]{1,0:T(8,128)(2,1)S(1)}, bf16[512,1024]{1,0:T(8,128)(2,1)S(1)}) fusion(bf16[512,4096]{1,0:T(8,128)(2,1)} %param.3, s32[]{:T(128)S(6)} %select_n.182, s32[]{:T(128)S(6)} %select_n.178, s32[]{:T(128)S(6)} %select_n.176, s32[]{:T(128)S(6)} %select_n.180), kind=kLoop, calls=%fused_computation.79 | loop fusion | bytes 8388624 | tf_op jit(solution)/shard_map/dynamic_slice | solution.py:145
  15.6 4.3 %collective-permute-start.3 = (bf16[512,1024]{1,0:T(8,128)(2,1)}, bf16[512,1024]{1,0:T(8,128)(2,1)S(1)}, u32[]{:S(2)}, u32[]{:S(2)}) collective-permute-start(bf16[512,1024]{1,0:T(8,128)(2,1)} %get-tuple-element.17), channel_id=1, source_target_pairs={{0,384},{16,400},{32,416},{48,432},{64,448},{80,464},{96,480},{112... | collective-permute-start | bytes 3145736 | tf_op jit(solution)/shard_map/ppermute | solution.py:146
  20.0 1.9 %collective-permute-start.1 = (bf16[512,1024]{1,0:T(8,128)(2,1)}, bf16[512,1024]{1,0:T(8,128)(2,1)}, u32[]{:S(2)}, u32[]{:S(2)}) collective-permute-start(bf16[512,1024]{1,0:T(8,128)(2,1)} %get-tuple-element.18), channel_id=1, source_target_pairs={{0,128},{16,144},{32,160},{48,176},{64,192},{80,208},{96,224},{112... | collective-permute-start | bytes 3145736 | tf_op jit(solution)/shard_map/ppermute | solution.py:146
  21.9 3.7 %collective-permute-start.2 = (bf16[512,1024]{1,0:T(8,128)(2,1)S(1)}, bf16[512,1024]{1,0:T(8,128)(2,1)}, u32[]{:S(2)}, u32[]{:S(2)}) collective-permute-start(bf16[512,1024]{1,0:T(8,128)(2,1)S(1)} %get-tuple-element.20), channel_id=1, source_target_pairs={{0,256},{16,272},{32,288},{48,304},{64,320},{80,336},{96,352},{112... | collective-permute-start | bytes 3145736 | tf_op jit(solution)/shard_map/ppermute | solution.py:146
  25.7 0.1 select_reduce_fusion
  25.8 6.9 %all-to-all-done = bf16[16,96,256]{2,1,0:T(8,128)(2,1)} async-done(((bf16[16,96,256]{2,1,0:T(8,128)(2,1)}), bf16[16,96,256]{2,1,0:T(8,128)(2,1)}, u32[]{:S(2)}, u32[]{:S(2)}) %all-to-all-start) | async-done | bytes 786464 | tf_op jit(solution)/shard_map/all_to_all | solution.py:141
  32.7 1.7 %fusion.2 = bf16[384,256]{1,0:T(8,128)(2,1)S(1)} fusion(bf16[1536,256]{1,0:T(8,128)(2,1)} %bitcast.2, s32[384]{0:T(512)S(1)} %fusion.14), kind=kOutput, calls=%fused_computation.4 | convolution fusion | flops 302678016 | bytes 984576 | tf_op jit(solution)/shard_map/dot_general | solution.py:157
  34.4 8.9 %collective-permute-start = (bf16[384,256]{1,0:T(8,128)(2,1)S(1)}, bf16[384,256]{1,0:T(8,128)(2,1)S(1)}, u32[]{:S(2)}, u32[]{:S(2)}) collective-permute-start(bf16[384,256]{1,0:T(8,128)(2,1)S(1)} %fusion.2), channel_id=1, source_target_pairs={{0,64},{16,80},{32,96},{48,112},{64,0},{80,16},{96,32},{112,48},{1... | collective-permute-start | bytes 589832 | tf_op jit(solution)/shard_map/ppermute | solution.py:160
  43.3 3.1 %multiply_reduce_fusion = f32[512]{0:T(512)S(1)} fusion(bf16[512,4096]{1,0:T(8,128)(2,1)} %param.3), kind=kLoop, calls=%fused_computation | loop fusion | flops 6290944 | bytes 4196352 | tf_op jit(solution)/shard_map/reduce_sum | solution.py:127
  46.4 12.3 %collective-permute-done = bf16[384,256]{1,0:T(8,128)(2,1)S(1)} collective-permute-done((bf16[384,256]{1,0:T(8,128)(2,1)S(1)}, bf16[384,256]{1,0:T(8,128)(2,1)S(1)}, u32[]{:S(2)}, u32[]{:S(2)}) %collective-permute-start) | collective-permute-done | bytes 196640 | tf_op jit(solution)/shard_map/ppermute | solution.py:160
  58.7 0.1 broadcast_select_fusion
  58.8 16.1 %all-gather = bf16[1536,256]{1,0:T(8,128)(2,1)S(1)} all-gather(bf16[384,256]{1,0:T(8,128)(2,1)S(1)} %broadcast_select_fusion), channel_id=2, replica_groups={{0,16,32,48},{64,80,96,112},{128,144,160,176},{192,208,224,240},{256,27..., dimensions={0}, use_global_device_ids=true | all-gather | bytes 983040 | tf_op jit(solution)/shard_map/all_gather | solution.py:164
  74.9 0.0 collective-permute-done.2.refs_2_
  74.9 4.8 %shard_map.38 = (f32[4,4,104,128]{3,2,1,0:T(8,128)S(1)}, f32[4,4,104,128]{3,2,1,0:T(8,128)S(1)}, f32[4,4,96,128]{3,2,1,0:T(8,128)S(1)}, f32[4,4,96,128]{3,2,1,0:T(8,128)S(1)}) custom-call(s32[1]{0:T(128)} %bitcast.y, bf16[4,384,256]{2,1,0:T(8,128)(2,1)S(1)} %bitcast.13, f32[8,128]{1,0:T(8,128)S(1)} %pad.4.store_sq, ...), custom_call_target="tpu_custom_call" | custom-call | flops 1610612736 | bytes 7340032 | tf_op jit(solution)/shard_map/pallas_call | solution.py:105
  79.7 4.1 %collective-permute-start.5 = (f32[4,4,104,128]{3,2,1,0:T(8,128)S(1)}, f32[4,4,104,128]{3,2,1,0:T(8,128)S(1)}, u32[]{:S(2)}, u32[]{:S(2)}) collective-permute-start(f32[4,4,104,128]{3,2,1,0:T(8,128)S(1)} %get-tuple-element.16), channel_id=1, source_target_pairs={{0,1},{1,0},{2,3},{3,2},{4,5},{5,4},{6,7},{7,6},{8,9},{9,8},{10,11... | collective-permute-start | bytes 2555912 | tf_op jit(solution)/shard_map/ppermute | solution.py:168
  83.8 2.0 %collective-permute-done.5 = f32[4,4,104,128]{3,2,1,0:T(8,128)S(1)} collective-permute-done((f32[4,4,104,128]{3,2,1,0:T(8,128)S(1)}, f32[4,4,104,128]{3,2,1,0:T(8,128)S(1)}, u32[]{:S(2)}, u32[]{:S(2)}) %collective-permute-start.5) | collective-permute-done | bytes 852000 | tf_op jit(solution)/shard_map/ppermute | solution.py:168
  85.8 1.0 add.224
  86.8 6.7 %all-to-all-start.2 = ((f32[16,104,128]{2,1,0:T(8,128)}), f32[16,104,128]{2,1,0:T(8,128)S(1)}, u32[]{:S(2)}, u32[]{:S(2)}) async-start(f32[16,104,128]{2,1,0:T(8,128)} %bitcast.6), calls=%async_computation.2 | async-start | bytes 1703936 | tf_op jit(solution)/shard_map/all_to_all | solution.py:170
  93.5 2.6 %collective-permute-start.4 = (f32[4,4,96,128]{3,2,1,0:T(8,128)}, f32[4,4,96,128]{3,2,1,0:T(8,128)S(1)}, u32[]{:S(2)}, u32[]{:S(2)}) collective-permute-start(f32[4,4,96,128]{3,2,1,0:T(8,128)} %copy-done), channel_id=1, source_target_pairs={{0,1},{1,0},{2,3},{3,2},{4,5},{5,4},{6,7},{7,6},{8,9},{9,8},{10,11... | collective-permute-start | bytes 2359304 | tf_op jit(solution)/shard_map/ppermute | solution.py:168
  96.1 2.1 %collective-permute-done.4 = f32[4,4,96,128]{3,2,1,0:T(8,128)S(1)} collective-permute-done((f32[4,4,96,128]{3,2,1,0:T(8,128)}, f32[4,4,96,128]{3,2,1,0:T(8,128)S(1)}, u32[]{:S(2)}, u32[]{:S(2)}) %collective-permute-start.4) | collective-permute-done | bytes 786464 | tf_op jit(solution)/shard_map/ppermute | solution.py:168
  98.2 1.0 add.223
  99.1 8.6 %all-to-all-done.2 = f32[16,104,128]{2,1,0:T(8,128)S(1)} async-done(((f32[16,104,128]{2,1,0:T(8,128)}), f32[16,104,128]{2,1,0:T(8,128)S(1)}, u32[]{:S(2)}, u32[]{:S(2)}) %all-to-all-start.2) | async-done | bytes 852000 | tf_op jit(solution)/shard_map/all_to_all | solution.py:170
  107.7 3.8 %all-to-all-start.1 = ((f32[16,96,128]{2,1,0:T(8,128)}), f32[16,96,128]{2,1,0:T(8,128)S(1)}, u32[]{:S(2)}, u32[]{:S(2)}) async-start(f32[16,96,128]{2,1,0:T(8,128)} %bitcast.14), calls=%async_computation.1 | async-start | bytes 1572864 | tf_op jit(solution)/shard_map/all_to_all | solution.py:170
  111.6 11.0 %collective-permute-start.6 = (f32[104,128]{1,0:T(8,128)S(1)}, f32[104,128]{1,0:T(8,128)S(1)}, u32[]{:S(2)}, u32[]{:S(2)}) collective-permute-start(f32[104,128]{1,0:T(8,128)S(1)} %reduce_sum.39), channel_id=1, source_target_pairs={{0,2},{1,3},{2,0},{3,1},{4,6},{5,7},{6,4},{7,5},{8,10},{9,11},{10,... | collective-permute-start | bytes 159752 | tf_op jit(solution)/shard_map/ppermute | solution.py:175
  122.5 1.6 %all-to-all-done.1 = f32[16,96,128]{2,1,0:T(8,128)S(1)} async-done(((f32[16,96,128]{2,1,0:T(8,128)}), f32[16,96,128]{2,1,0:T(8,128)S(1)}, u32[]{:S(2)}, u32[]{:S(2)}) %all-to-all-start.1) | async-done | bytes 786464 | tf_op jit(solution)/shard_map/all_to_all | solution.py:170
  124.2 1.0 collective-permute-done.6
  125.2 0.1 rsqrt.15
  125.3 0.1 fusion.5
  125.4 0.7 reshape.183
  (14 shorter events, 0.2 us)
Async XLA Ops:
  2.1 30.6 %all-to-all-start = ((bf16[16,96,256]{2,1,0:T(8,128)(2,1)}), bf16[16,96,256]{2,1,0:T(8,128)(2,1)}, u32[]{:S(2)}, u32[]{:S(2)}) async-start(bf16[16,96,256]{2,1,0:T(8,128)(2,1)} %shard_map.37), calls=%async_computation | async-start | bytes 1572864 | tf_op jit(solution)/shard_map/all_to_all | solution.py:141
  11.4 14.2 %copy-start.1 = (s32[4]{0:T(128)S(1)}, s32[4]{0:T(128)}, u32[]{:S(2)}) copy-start(s32[4]{0:T(128)} %param.5) | copy-start | bytes 52
  15.6 59.3 %collective-permute-start.3 = (bf16[512,1024]{1,0:T(8,128)(2,1)}, bf16[512,1024]{1,0:T(8,128)(2,1)S(1)}, u32[]{:S(2)}, u32[]{:S(2)}) collective-permute-start(bf16[512,1024]{1,0:T(8,128)(2,1)} %get-tuple-element.17), channel_id=1, source_target_pairs={{0,384},{16,400},{32,416},{48,432},{64,448},{80,464},{96,480},{112... | collective-permute-start | bytes 3145736 | tf_op jit(solution)/shard_map/ppermute | solution.py:146
  20.0 54.9 %collective-permute-start.1 = (bf16[512,1024]{1,0:T(8,128)(2,1)}, bf16[512,1024]{1,0:T(8,128)(2,1)}, u32[]{:S(2)}, u32[]{:S(2)}) collective-permute-start(bf16[512,1024]{1,0:T(8,128)(2,1)} %get-tuple-element.18), channel_id=1, source_target_pairs={{0,128},{16,144},{32,160},{48,176},{64,192},{80,208},{96,224},{112... | collective-permute-start | bytes 3145736 | tf_op jit(solution)/shard_map/ppermute | solution.py:146
  21.9 53.0 %collective-permute-start.2 = (bf16[512,1024]{1,0:T(8,128)(2,1)S(1)}, bf16[512,1024]{1,0:T(8,128)(2,1)}, u32[]{:S(2)}, u32[]{:S(2)}) collective-permute-start(bf16[512,1024]{1,0:T(8,128)(2,1)S(1)} %get-tuple-element.20), channel_id=1, source_target_pairs={{0,256},{16,272},{32,288},{48,304},{64,320},{80,336},{96,352},{112... | collective-permute-start | bytes 3145736 | tf_op jit(solution)/shard_map/ppermute | solution.py:146
  34.4 24.2 %collective-permute-start = (bf16[384,256]{1,0:T(8,128)(2,1)S(1)}, bf16[384,256]{1,0:T(8,128)(2,1)S(1)}, u32[]{:S(2)}, u32[]{:S(2)}) collective-permute-start(bf16[384,256]{1,0:T(8,128)(2,1)S(1)} %fusion.2), channel_id=1, source_target_pairs={{0,64},{16,80},{32,96},{48,112},{64,0},{80,16},{96,32},{112,48},{1... | collective-permute-start | bytes 589832 | tf_op jit(solution)/shard_map/ppermute | solution.py:160
  79.7 7.1 %copy-start = (f32[4,4,96,128]{3,2,1,0:T(8,128)}, f32[4,4,96,128]{3,2,1,0:T(8,128)S(1)}, u32[]{:S(2)}) copy-start(f32[4,4,96,128]{3,2,1,0:T(8,128)S(1)} %get-tuple-element.14) | copy-start | bytes 2359300
  79.7 6.1 %collective-permute-start.5 = (f32[4,4,104,128]{3,2,1,0:T(8,128)S(1)}, f32[4,4,104,128]{3,2,1,0:T(8,128)S(1)}, u32[]{:S(2)}, u32[]{:S(2)}) collective-permute-start(f32[4,4,104,128]{3,2,1,0:T(8,128)S(1)} %get-tuple-element.16), channel_id=1, source_target_pairs={{0,1},{1,0},{2,3},{3,2},{4,5},{5,4},{6,7},{7,6},{8,9},{9,8},{10,11... | collective-permute-start | bytes 2555912 | tf_op jit(solution)/shard_map/ppermute | solution.py:168
  86.8 20.9 %all-to-all-start.2 = ((f32[16,104,128]{2,1,0:T(8,128)}), f32[16,104,128]{2,1,0:T(8,128)S(1)}, u32[]{:S(2)}, u32[]{:S(2)}) async-start(f32[16,104,128]{2,1,0:T(8,128)} %bitcast.6), calls=%async_computation.2 | async-start | bytes 1703936 | tf_op jit(solution)/shard_map/all_to_all | solution.py:170
  93.5 4.7 %collective-permute-start.4 = (f32[4,4,96,128]{3,2,1,0:T(8,128)}, f32[4,4,96,128]{3,2,1,0:T(8,128)S(1)}, u32[]{:S(2)}, u32[]{:S(2)}) collective-permute-start(f32[4,4,96,128]{3,2,1,0:T(8,128)} %copy-done), channel_id=1, source_target_pairs={{0,1},{1,0},{2,3},{3,2},{4,5},{5,4},{6,7},{7,6},{8,9},{9,8},{10,11... | collective-permute-start | bytes 2359304 | tf_op jit(solution)/shard_map/ppermute | solution.py:168
  107.7 16.4 %all-to-all-start.1 = ((f32[16,96,128]{2,1,0:T(8,128)}), f32[16,96,128]{2,1,0:T(8,128)S(1)}, u32[]{:S(2)}, u32[]{:S(2)}) async-start(f32[16,96,128]{2,1,0:T(8,128)} %bitcast.14), calls=%async_computation.1 | async-start | bytes 1572864 | tf_op jit(solution)/shard_map/all_to_all | solution.py:170
  111.6 13.6 %collective-permute-start.6 = (f32[104,128]{1,0:T(8,128)S(1)}, f32[104,128]{1,0:T(8,128)S(1)}, u32[]{:S(2)}, u32[]{:S(2)}) collective-permute-start(f32[104,128]{1,0:T(8,128)S(1)} %reduce_sum.39), channel_id=1, source_target_pairs={{0,2},{1,3},{2,0},{3,1},{4,6},{5,7},{6,4},{7,5},{8,10},{9,11},{10,... | collective-permute-start | bytes 159752 | tf_op jit(solution)/shard_map/ppermute | solution.py:175

commit v4 on v3

--- a/solution.py
+++ b/solution.py
@@ -28,20 +28,26 @@
     return [(y * NZ + z, (y + step) % NY * NZ + z) for y in range(NY) for z in range(NZ)]
 
 
-def cut_kernel(block, out):
+def cut_kernel(block, out, done):
     width = out.shape[2]
-    for part in range(out.shape[0]):
-        out[part] = block[:, part * width : (part + 1) * width]
+    copies = [
+        pltpu.make_async_copy(block.at[:, pl.ds(part * width, width)], out.at[part], done.at[part])
+        for part in range(out.shape[0])
+    ]
+    for copy in copies:
+        copy.start()
+    for copy in copies:
+        copy.wait()
 
 
 def cut_columns(block, parts):
     rows, cols = block.shape
-    vmem = pl.BlockSpec(memory_space=pltpu.VMEM)
     return pl.pallas_call(
         cut_kernel,
-        in_specs=[vmem],
-        out_specs=vmem,
+        in_specs=[pl.BlockSpec(memory_space=pl.ANY)],
+        out_specs=pl.BlockSpec(memory_space=pltpu.VMEM),
         out_shape=jax.ShapeDtypeStruct((parts, rows, cols // parts), block.dtype),
+        scratch_shapes=[pltpu.SemaphoreType.DMA((parts,))],
     )(block)
 
 

time: 128 us -> 128 us (level)
  no operation moved by 1% of the time
where the time goes in v4:
time: 128 us; the launch traced here: 126 us
  starting transfers between devices  56.1 us (44%)
  waiting for transfers between devices  34.5 us (27%)
  blocking collectives  16.1 us (13%)
  Pallas kernels  6.96 us (5%)
  other arithmetic  5.57 us (4%)
  local copies, waits for them, and re-layouts  4.93 us (4%)
  matrix products  1.7 us (1%)
    all_gather x1, blocking collectives, per_device(): chosen = lax.all_gather(piece, 'row', axis_index_groups=QUADS)  16.1 us
    ppermute x1, waiting for transfers between devices, per_device(): other = lax.ppermute(piece, 'row', CROSS)  12.3 us
    ppermute x1, starting transfers between devices, per_device(): got = lax.ppermute(give, 'width', SWAP_H)  11 us
    all_to_all x2, starting transfers between devices, summed(): lax.all_to_all(total, ('row', 'width'), 0, 0, axis_index_groups=PLANES)  10.4 us
    all_to_all x2, waiting for transfers between devices, summed(): lax.all_to_all(total, ('row', 'width'), 0, 0, axis_index_groups=PLANES)  10.2 us
    ppermute x3, starting transfers between devices, per_device(): stores.append(lax.ppermute(part, 'row', turn(step)) if step else part)  9.9 us
    all_to_all x1, starting transfers between devices, per_device(): parts = lax.all_to_all(parts, 'row', 0, 0, axis_index_groups=SQUARES)  9.24 us
    ppermute x1, starting transfers between devices, per_device(): other = lax.ppermute(piece, 'row', CROSS)  8.88 us
  transfers between devices with their start and end apart: 10, of which 7 were waited for; matrix products, arithmetic and copies ran while one was open for 8% of the time, Pallas kernels for 0%

profile of v4, /device:TPU:1, one launch (start us, length us, event | category | flops | bytes accessed | tf_op | source)
XLA Modules:
  0.0 126.2 jit_solution(11271155452072524407)
XLA Ops:
  0.0 2.2 %shard_map.37 = bf16[16,96,256]{2,1,0:T(8,128)(2,1)} custom-call(bf16[96,4096]{1,0:T(8,128)(2,1)} %bitcast.15), custom_call_target="tpu_custom_call" | custom-call | tf_op jit(solution)/shard_map/pallas_call | solution.py:45
  2.2 9.2 %all-to-all-start = ((bf16[16,96,256]{2,1,0:T(8,128)(2,1)}), bf16[16,96,256]{2,1,0:T(8,128)(2,1)}, u32[]{:S(2)}, u32[]{:S(2)}) async-start(bf16[16,96,256]{2,1,0:T(8,128)(2,1)} %shard_map.37), calls=%async_computation | async-start | bytes 1572864 | tf_op jit(solution)/shard_map/all_to_all | solution.py:147
  11.6 0.0 copy-start.1
  11.6 4.2 %constant_dynamic-slice_fusion.3 = (bf16[512,1024]{1,0:T(8,128)(2,1)}, bf16[512,1024]{1,0:T(8,128)(2,1)}, bf16[512,1024]{1,0:T(8,128)(2,1)S(1)}, bf16[512,1024]{1,0:T(8,128)(2,1)S(1)}) fusion(bf16[512,4096]{1,0:T(8,128)(2,1)} %param.3, s32[]{:T(128)S(6)} %select_n.182, s32[]{:T(128)S(6)} %select_n.178, s32[]{:T(128)S(6)} %select_n.176, s32[]{:T(128)S(6)} %select_n.180), kind=kLoop, calls=%fused_computation.79 | loop fusion | bytes 8388624 | tf_op jit(solution)/shard_map/dynamic_slice | solution.py:151
  15.7 4.3 %collective-permute-start.3 = (bf16[512,1024]{1,0:T(8,128)(2,1)}, bf16[512,1024]{1,0:T(8,128)(2,1)S(1)}, u32[]{:S(2)}, u32[]{:S(2)}) collective-permute-start(bf16[512,1024]{1,0:T(8,128)(2,1)} %get-tuple-element.17), channel_id=1, source_target_pairs={{0,384},{16,400},{32,416},{48,432},{64,448},{80,464},{96,480},{112... | collective-permute-start | bytes 3145736 | tf_op jit(solution)/shard_map/ppermute | solution.py:152
  20.1 1.9 %collective-permute-start.1 = (bf16[512,1024]{1,0:T(8,128)(2,1)}, bf16[512,1024]{1,0:T(8,128)(2,1)}, u32[]{:S(2)}, u32[]{:S(2)}) collective-permute-start(bf16[512,1024]{1,0:T(8,128)(2,1)} %get-tuple-element.18), channel_id=1, source_target_pairs={{0,128},{16,144},{32,160},{48,176},{64,192},{80,208},{96,224},{112... | collective-permute-start | bytes 3145736 | tf_op jit(solution)/shard_map/ppermute | solution.py:152
  22.0 3.7 %collective-permute-start.2 = (bf16[512,1024]{1,0:T(8,128)(2,1)S(1)}, bf16[512,1024]{1,0:T(8,128)(2,1)}, u32[]{:S(2)}, u32[]{:S(2)}) collective-permute-start(bf16[512,1024]{1,0:T(8,128)(2,1)S(1)} %get-tuple-element.20), channel_id=1, source_target_pairs={{0,256},{16,272},{32,288},{48,304},{64,320},{80,336},{96,352},{112... | collective-permute-start | bytes 3145736 | tf_op jit(solution)/shard_map/ppermute | solution.py:152
  25.8 0.1 select_reduce_fusion
  25.9 6.9 %all-to-all-done = bf16[16,96,256]{2,1,0:T(8,128)(2,1)} async-done(((bf16[16,96,256]{2,1,0:T(8,128)(2,1)}), bf16[16,96,256]{2,1,0:T(8,128)(2,1)}, u32[]{:S(2)}, u32[]{:S(2)}) %all-to-all-start) | async-done | bytes 786464 | tf_op jit(solution)/shard_map/all_to_all | solution.py:147
  32.8 1.7 %fusion.2 = bf16[384,256]{1,0:T(8,128)(2,1)S(1)} fusion(bf16[1536,256]{1,0:T(8,128)(2,1)} %bitcast.2, s32[384]{0:T(512)S(1)} %fusion.14), kind=kOutput, calls=%fused_computation.4 | convolution fusion | flops 302678016 | bytes 984576 | tf_op jit(solution)/shard_map/dot_general | solution.py:163
  34.5 8.9 %collective-permute-start = (bf16[384,256]{1,0:T(8,128)(2,1)S(1)}, bf16[384,256]{1,0:T(8,128)(2,1)S(1)}, u32[]{:S(2)}, u32[]{:S(2)}) collective-permute-start(bf16[384,256]{1,0:T(8,128)(2,1)S(1)} %fusion.2), channel_id=1, source_target_pairs={{0,64},{16,80},{32,96},{48,112},{64,0},{80,16},{96,32},{112,48},{1... | collective-permute-start | bytes 589832 | tf_op jit(solution)/shard_map/ppermute | solution.py:166
  43.4 3.1 %multiply_reduce_fusion = f32[512]{0:T(512)S(1)} fusion(bf16[512,4096]{1,0:T(8,128)(2,1)} %param.3), kind=kLoop, calls=%fused_computation | loop fusion | flops 6290944 | bytes 4196352 | tf_op jit(solution)/shard_map/reduce_sum | solution.py:133
  46.5 12.3 %collective-permute-done = bf16[384,256]{1,0:T(8,128)(2,1)S(1)} collective-permute-done((bf16[384,256]{1,0:T(8,128)(2,1)S(1)}, bf16[384,256]{1,0:T(8,128)(2,1)S(1)}, u32[]{:S(2)}, u32[]{:S(2)}) %collective-permute-start) | collective-permute-done | bytes 196640 | tf_op jit(solution)/shard_map/ppermute | solution.py:166
  58.8 0.1 broadcast_select_fusion
  58.9 16.1 %all-gather = bf16[1536,256]{1,0:T(8,128)(2,1)S(1)} all-gather(bf16[384,256]{1,0:T(8,128)(2,1)S(1)} %broadcast_select_fusion), channel_id=2, replica_groups={{0,16,32,48},{64,80,96,112},{128,144,160,176},{192,208,224,240},{256,27..., dimensions={0}, use_global_device_ids=true | all-gather | bytes 983040 | tf_op jit(solution)/shard_map/all_gather | solution.py:170
  75.0 0.0 collective-permute-done.2.refs_2_
  75.0 4.8 %shard_map.38 = (f32[4,4,104,128]{3,2,1,0:T(8,128)S(1)}, f32[4,4,104,128]{3,2,1,0:T(8,128)S(1)}, f32[4,4,96,128]{3,2,1,0:T(8,128)S(1)}, f32[4,4,96,128]{3,2,1,0:T(8,128)S(1)}) custom-call(s32[1]{0:T(128)} %bitcast.y, bf16[4,384,256]{2,1,0:T(8,128)(2,1)S(1)} %bitcast.13, f32[8,128]{1,0:T(8,128)S(1)} %pad.4.store_sq, ...), custom_call_target="tpu_custom_call" | custom-call | flops 1610612736 | bytes 7340032 | tf_op jit(solution)/shard_map/pallas_call | solution.py:111
  79.8 4.1 %collective-permute-start.5 = (f32[4,4,104,128]{3,2,1,0:T(8,128)S(1)}, f32[4,4,104,128]{3,2,1,0:T(8,128)S(1)}, u32[]{:S(2)}, u32[]{:S(2)}) collective-permute-start(f32[4,4,104,128]{3,2,1,0:T(8,128)S(1)} %get-tuple-element.16), channel_id=1, source_target_pairs={{0,1},{1,0},{2,3},{3,2},{4,5},{5,4},{6,7},{7,6},{8,9},{9,8},{10,11... | collective-permute-start | bytes 2555912 | tf_op jit(solution)/shard_map/ppermute | solution.py:174
  83.9 2.0 %collective-permute-done.5 = f32[4,4,104,128]{3,2,1,0:T(8,128)S(1)} collective-permute-done((f32[4,4,104,128]{3,2,1,0:T(8,128)S(1)}, f32[4,4,104,128]{3,2,1,0:T(8,128)S(1)}, u32[]{:S(2)}, u32[]{:S(2)}) %collective-permute-start.5) | collective-permute-done | bytes 852000 | tf_op jit(solution)/shard_map/ppermute | solution.py:174
  85.9 1.0 add.224
  86.9 6.7 %all-to-all-start.2 = ((f32[16,104,128]{2,1,0:T(8,128)}), f32[16,104,128]{2,1,0:T(8,128)S(1)}, u32[]{:S(2)}, u32[]{:S(2)}) async-start(f32[16,104,128]{2,1,0:T(8,128)} %bitcast.6), calls=%async_computation.2 | async-start | bytes 1703936 | tf_op jit(solution)/shard_map/all_to_all | solution.py:176
  93.6 2.6 %collective-permute-start.4 = (f32[4,4,96,128]{3,2,1,0:T(8,128)}, f32[4,4,96,128]{3,2,1,0:T(8,128)S(1)}, u32[]{:S(2)}, u32[]{:S(2)}) collective-permute-start(f32[4,4,96,128]{3,2,1,0:T(8,128)} %copy-done), channel_id=1, source_target_pairs={{0,1},{1,0},{2,3},{3,2},{4,5},{5,4},{6,7},{7,6},{8,9},{9,8},{10,11... | collective-permute-start | bytes 2359304 | tf_op jit(solution)/shard_map/ppermute | solution.py:174
  96.2 2.1 %collective-permute-done.4 = f32[4,4,96,128]{3,2,1,0:T(8,128)S(1)} collective-permute-done((f32[4,4,96,128]{3,2,1,0:T(8,128)}, f32[4,4,96,128]{3,2,1,0:T(8,128)S(1)}, u32[]{:S(2)}, u32[]{:S(2)}) %collective-permute-start.4) | collective-permute-done | bytes 786464 | tf_op jit(solution)/shard_map/ppermute | solution.py:174
  98.3 1.0 add.223
  99.2 8.6 %all-to-all-done.2 = f32[16,104,128]{2,1,0:T(8,128)S(1)} async-done(((f32[16,104,128]{2,1,0:T(8,128)}), f32[16,104,128]{2,1,0:T(8,128)S(1)}, u32[]{:S(2)}, u32[]{:S(2)}) %all-to-all-start.2) | async-done | bytes 852000 | tf_op jit(solution)/shard_map/all_to_all | solution.py:176
  107.8 3.8 %all-to-all-start.1 = ((f32[16,96,128]{2,1,0:T(8,128)}), f32[16,96,128]{2,1,0:T(8,128)S(1)}, u32[]{:S(2)}, u32[]{:S(2)}) async-start(f32[16,96,128]{2,1,0:T(8,128)} %bitcast.14), calls=%async_computation.1 | async-start | bytes 1572864 | tf_op jit(solution)/shard_map/all_to_all | solution.py:176
  111.7 11.0 %collective-permute-start.6 = (f32[104,128]{1,0:T(8,128)S(1)}, f32[104,128]{1,0:T(8,128)S(1)}, u32[]{:S(2)}, u32[]{:S(2)}) collective-permute-start(f32[104,128]{1,0:T(8,128)S(1)} %reduce_sum.39), channel_id=1, source_target_pairs={{0,2},{1,3},{2,0},{3,1},{4,6},{5,7},{6,4},{7,5},{8,10},{9,11},{10,... | collective-permute-start | bytes 159752 | tf_op jit(solution)/shard_map/ppermute | solution.py:181
  122.6 1.6 %all-to-all-done.1 = f32[16,96,128]{2,1,0:T(8,128)S(1)} async-done(((f32[16,96,128]{2,1,0:T(8,128)}), f32[16,96,128]{2,1,0:T(8,128)S(1)}, u32[]{:S(2)}, u32[]{:S(2)}) %all-to-all-start.1) | async-done | bytes 786464 | tf_op jit(solution)/shard_map/all_to_all | solution.py:176
  124.3 1.0 collective-permute-done.6
  125.3 0.1 rsqrt.15
  125.4 0.1 fusion.5
  125.5 0.7 reshape.183
  (14 shorter events, 0.2 us)
Async XLA Ops:
  2.2 30.6 %all-to-all-start = ((bf16[16,96,256]{2,1,0:T(8,128)(2,1)}), bf16[16,96,256]{2,1,0:T(8,128)(2,1)}, u32[]{:S(2)}, u32[]{:S(2)}) async-start(bf16[16,96,256]{2,1,0:T(8,128)(2,1)} %shard_map.37), calls=%async_computation | async-start | bytes 1572864 | tf_op jit(solution)/shard_map/all_to_all | solution.py:147
  11.6 14.2 %copy-start.1 = (s32[4]{0:T(128)S(1)}, s32[4]{0:T(128)}, u32[]{:S(2)}) copy-start(s32[4]{0:T(128)} %param.5) | copy-start | bytes 52
  15.7 59.3 %collective-permute-start.3 = (bf16[512,1024]{1,0:T(8,128)(2,1)}, bf16[512,1024]{1,0:T(8,128)(2,1)S(1)}, u32[]{:S(2)}, u32[]{:S(2)}) collective-permute-start(bf16[512,1024]{1,0:T(8,128)(2,1)} %get-tuple-element.17), channel_id=1, source_target_pairs={{0,384},{16,400},{32,416},{48,432},{64,448},{80,464},{96,480},{112... | collective-permute-start | bytes 3145736 | tf_op jit(solution)/shard_map/ppermute | solution.py:152
  20.1 54.9 %collective-permute-start.1 = (bf16[512,1024]{1,0:T(8,128)(2,1)}, bf16[512,1024]{1,0:T(8,128)(2,1)}, u32[]{:S(2)}, u32[]{:S(2)}) collective-permute-start(bf16[512,1024]{1,0:T(8,128)(2,1)} %get-tuple-element.18), channel_id=1, source_target_pairs={{0,128},{16,144},{32,160},{48,176},{64,192},{80,208},{96,224},{112... | collective-permute-start | bytes 3145736 | tf_op jit(solution)/shard_map/ppermute | solution.py:152
  22.0 53.0 %collective-permute-start.2 = (bf16[512,1024]{1,0:T(8,128)(2,1)S(1)}, bf16[512,1024]{1,0:T(8,128)(2,1)}, u32[]{:S(2)}, u32[]{:S(2)}) collective-permute-start(bf16[512,1024]{1,0:T(8,128)(2,1)S(1)} %get-tuple-element.20), channel_id=1, source_target_pairs={{0,256},{16,272},{32,288},{48,304},{64,320},{80,336},{96,352},{112... | collective-permute-start | bytes 3145736 | tf_op jit(solution)/shard_map/ppermute | solution.py:152
  34.5 24.2 %collective-permute-start = (bf16[384,256]{1,0:T(8,128)(2,1)S(1)}, bf16[384,256]{1,0:T(8,128)(2,1)S(1)}, u32[]{:S(2)}, u32[]{:S(2)}) collective-permute-start(bf16[384,256]{1,0:T(8,128)(2,1)S(1)} %fusion.2), channel_id=1, source_target_pairs={{0,64},{16,80},{32,96},{48,112},{64,0},{80,16},{96,32},{112,48},{1... | collective-permute-start | bytes 589832 | tf_op jit(solution)/shard_map/ppermute | solution.py:166
  79.8 7.1 %copy-start = (f32[4,4,96,128]{3,2,1,0:T(8,128)}, f32[4,4,96,128]{3,2,1,0:T(8,128)S(1)}, u32[]{:S(2)}) copy-start(f32[4,4,96,128]{3,2,1,0:T(8,128)S(1)} %get-tuple-element.14) | copy-start | bytes 2359300
  79.8 6.1 %collective-permute-start.5 = (f32[4,4,104,128]{3,2,1,0:T(8,128)S(1)}, f32[4,4,104,128]{3,2,1,0:T(8,128)S(1)}, u32[]{:S(2)}, u32[]{:S(2)}) collective-permute-start(f32[4,4,104,128]{3,2,1,0:T(8,128)S(1)} %get-tuple-element.16), channel_id=1, source_target_pairs={{0,1},{1,0},{2,3},{3,2},{4,5},{5,4},{6,7},{7,6},{8,9},{9,8},{10,11... | collective-permute-start | bytes 2555912 | tf_op jit(solution)/shard_map/ppermute | solution.py:174
  86.9 20.9 %all-to-all-start.2 = ((f32[16,104,128]{2,1,0:T(8,128)}), f32[16,104,128]{2,1,0:T(8,128)S(1)}, u32[]{:S(2)}, u32[]{:S(2)}) async-start(f32[16,104,128]{2,1,0:T(8,128)} %bitcast.6), calls=%async_computation.2 | async-start | bytes 1703936 | tf_op jit(solution)/shard_map/all_to_all | solution.py:176
  93.6 4.7 %collective-permute-start.4 = (f32[4,4,96,128]{3,2,1,0:T(8,128)}, f32[4,4,96,128]{3,2,1,0:T(8,128)S(1)}, u32[]{:S(2)}, u32[]{:S(2)}) collective-permute-start(f32[4,4,96,128]{3,2,1,0:T(8,128)} %copy-done), channel_id=1, source_target_pairs={{0,1},{1,0},{2,3},{3,2},{4,5},{5,4},{6,7},{7,6},{8,9},{9,8},{10,11... | collective-permute-start | bytes 2359304 | tf_op jit(solution)/shard_map/ppermute | solution.py:174
  107.8 16.4 %all-to-all-start.1 = ((f32[16,96,128]{2,1,0:T(8,128)}), f32[16,96,128]{2,1,0:T(8,128)S(1)}, u32[]{:S(2)}, u32[]{:S(2)}) async-start(f32[16,96,128]{2,1,0:T(8,128)} %bitcast.14), calls=%async_computation.1 | async-start | bytes 1572864 | tf_op jit(solution)/shard_map/all_to_all | solution.py:176
  111.7 13.6 %collective-permute-start.6 = (f32[104,128]{1,0:T(8,128)S(1)}, f32[104,128]{1,0:T(8,128)S(1)}, u32[]{:S(2)}, u32[]{:S(2)}) collective-permute-start(f32[104,128]{1,0:T(8,128)S(1)} %reduce_sum.39), channel_id=1, source_target_pairs={{0,2},{1,3},{2,0},{3,1},{4,6},{5,7},{6,4},{7,5},{8,10},{9,11},{10,... | collective-permute-start | bytes 159752 | tf_op jit(solution)/shard_map/ppermute | solution.py:181
